TPU v7x, 32 devices: a whole 2x2x4 slice. The times are simulated.
32 devices in a mesh: tile: 16 (over z, y, core), layer: 2 (over x).
Axes of the slice: x: 2, y: 2, z: 4, core: 2. Of those that a mesh axis runs over, the one named last changes fastest.
Arguments:
- ensemble: float32 [64, 8, 8192], P(None, 'layer', 'tile'), may hold values from -6 to 6
- diff_x: float32 [8, 8192], P('layer', 'tile'), may hold values from 0.04 to 0.2
- diff_z: float32 [8, 8192], P('layer', 'tile'), may hold values from 0.04 to 0.2
- cour_x: float32 [8, 8192], P('layer', 'tile'), may hold values from -0.4 to 0.4
- cour_z: float32 [8, 8192], P('layer', 'tile'), may hold values from -0.4 to 0.4
- obs_cell: int32 [4, 512], replicated, may hold values from 0 to 65535
- obs_radius: int32 [4, 512], replicated, may hold values from 2048 to 8192
- obs_value: float32 [4, 512], replicated, may hold values from -6 to 6
- obs_var: float32 [4, 512], replicated, may hold values from 0.1 to 1
Outputs:
- posterior: float32 [64, 8, 8192], P(None, 'layer', 'tile')
Inputs may be any that keep to these rules, and one draw needn't show every extreme that they name: `obs_cell`: cells are drawn independently over the whole grid; two observations may share a cell.
All inputs are finite; a program needn't handle non-finite values.
Results may differ from a plain program's by a relative error of at most 0.00019.
Values sent between devices are 32-bit elements; how exact they have to be, the bound alone decides.
A program may use at most 64 MiB of HBM per device.

v0:
```python
import functools

import jax
import jax.numpy as jnp
from jax import lax
from jax.experimental import pallas as pl
from jax.experimental.pallas import tpu as pltpu
from jax.sharding import PartitionSpec as P

MESH = pl.DeviceIdType.MESH
LANES = 128


def split_cell(cells, total):
    if total & (total - 1) == 0:
        return cells >> (total.bit_length() - 1), cells & (total - 1)
    return cells // total, cells % total


def halves(value):
    high = value.astype(jnp.bfloat16)
    return high, (value - high.astype(jnp.float32)).astype(jnp.bfloat16)


def gather_kernel(
    tiles, layers, ens_in, dx_in, dz_in, cx_in, cz_in, cell_in, state_out, prior,
    state, state_sem, ens, diff_x, diff_z, cour_x, cour_z, obs_cell, load_sem,
    cells, edge_w, edge_e, halo_w, halo_e, halo_u, halo_d, coef_up, coef_down, coef_u, coef_d,
    part, in_core, in_plane, in_line, halo_send, halo_recv, core_sem, plane_send, plane_recv, line_send, line_recv,
):
    loads = []
    for i, (src, dst) in enumerate(
        ((ens_in, ens), (dz_in, diff_z), (cz_in, cour_z), (dx_in, diff_x), (cx_in, cour_x), (cell_in, obs_cell))
    ):
        copy = pltpu.make_async_copy(src, dst, load_sem.at[i])
        copy.start()
        loads.append(copy)
    members, depth, width = ens.shape
    batches, count = obs_cell.shape
    tile, layer = lax.axis_index("tile"), lax.axis_index("layer")
    core, row, line = tile % 2, (tile // 2) % 2, tile // 4
    plane_n, line_n = layers * 2, tiles // 4
    spot = layer * 2 + row
    pair = (tile + 1 - 2 * core, layer)

    def plane_at(index):
        return (line * 4 + (index % 2) * 2 + core, index // 2)

    def line_at(index):
        return (index * 4 + row * 2 + core, layer)

    greeted = [pair, ((tile + 1) % tiles, layer), ((tile + tiles - 1) % tiles, layer)]
    greeted += [(tile, (layer + 1) % layers), (tile, (layer + layers - 1) % layers)]
    greeted += [plane_at((spot + j) % plane_n) for j in range(1, plane_n)]
    greeted += [line_at((line + j) % line_n) for j in range(1, line_n)]
    barrier = pltpu.get_barrier_semaphore()
    for device in greeted:
        pl.semaphore_signal(barrier, inc=1, device_id=device, device_id_type=MESH)

    for copy in loads:
        copy.wait()
    lane = lax.broadcasted_iota(jnp.int32, (members, LANES), 1)
    west = jnp.zeros((members, LANES), jnp.float32)
    east = jnp.zeros((members, LANES), jnp.float32)
    for l in range(depth):
        x = ens[:, l, :]
        cells[l] = x
        west = jnp.where(lane == l, x[:, 0:1], west)
        east = jnp.where(lane == l, x[:, width - 1 : width], east)
    edge_w[...] = west
    edge_e[...] = east
    tall = coef_up.shape
    coef_up[...] = jnp.broadcast_to(diff_z[0:1, :] + 0.5 * cour_z[0:1, :], tall)
    coef_down[...] = jnp.broadcast_to(diff_z[depth - 1 : depth, :] - 0.5 * cour_z[depth - 1 : depth, :], tall)
    pl.semaphore_wait(barrier, len(greeted))

    def remote(src, dst, send, recv, device):
        return pltpu.make_async_remote_copy(
            src_ref=src, dst_ref=dst, send_sem=send, recv_sem=recv, device_id=device, device_id_type=MESH
        )

    up, down = layer > 0, layer < layers - 1
    before, after = tile > 0, tile < tiles - 1
    above, below = (tile, lax.rem(layer + layers - 1, layers)), (tile, lax.rem(layer + 1, layers))
    ahead, behind = (lax.rem(tile + 1, tiles), layer), (lax.rem(tile + tiles - 1, tiles), layer)

    def move(i, sends, receives, src, dst, device):
        return sends, receives, remote(src, dst, halo_send.at[i], halo_recv.at[i], device), dst

    small = (
        move(0, after, before, edge_e, halo_w, ahead),
        move(1, before, after, edge_w, halo_e, behind),
        move(2, down, up, coef_down, coef_u, below),
        move(3, up, down, coef_up, coef_d, above),
    )
    large = (
        move(4, down, up, cells.at[depth - 1], halo_u, below),
        move(5, up, down, cells.at[0], halo_d, above),
    )
    for sends, receives, copy, place in small:
        pl.when(sends)(copy.start)
    for sends, receives, copy, place in small + large:

        @pl.when(jnp.logical_not(receives))
        def _(place=place):
            place[...] = jnp.zeros_like(place)

    for sends, receives, copy, place in small:
        pl.when(receives)(copy.wait_recv)

    column = lax.broadcasted_iota(jnp.int32, (members, width), 1)
    levels = list(range(depth)) + [-1, depth]
    parts = []
    for l in range(depth):
        x = cells[l]
        left = jnp.where(column == 0, halo_w[:, l : l + 1], pltpu.roll(x, 1, 1))
        right = jnp.where(column == width - 1, halo_e[:, l : l + 1], pltpu.roll(x, width - 1, 1))
        dx, dz = diff_x[l : l + 1, :], diff_z[l : l + 1, :]
        cx, cz = 0.5 * cour_x[l : l + 1, :], 0.5 * cour_z[l : l + 1, :]
        new = x * (1.0 - 2.0 * dz - 2.0 * dx) + left * (dx + cx) + right * (dx - cx)
        if l > 0:
            new = new + cells[l - 1] * (dz + cz)
        if l < depth - 1:
            new = new + cells[l + 1] * (dz - cz)
        state[l] = new
        parts.extend(halves(new))
    parts.extend(halves(cells[0] * coef_u[0:1, :]))
    parts.extend(halves(cells[depth - 1] * coef_d[0:1, :]))
    stacked = jnp.concatenate(parts, axis=0)

    blocks = count // LANES
    extent = blocks * members
    half = extent // 2
    size = half // plane_n
    scatter = size % (8 * line_n) == 0
    piece = size // line_n if scatter else size
    place = lax.broadcasted_iota(jnp.int32, (width, count), 0)

    def start_of(b, *steps):
        total = b * extent
        for index, length in steps:
            total = total + index * length
        return pl.multiple_of(total, 8)

    every = range(batches)
    core_out, plane_out, line_out, line_back, plane_back, core_back = ([[] for _ in every] for _ in range(6))
    for b in every:
        rows, cols = split_cell(obs_cell[b : b + 1, :], tiles * width)
        rows, cols = rows - layer * depth, cols - tile * width
        hot = jnp.where(place == cols, 1.0, 0.0).astype(jnp.bfloat16)
        picked = jnp.dot(stacked, hot, preferred_element_type=jnp.float32)
        total = jnp.zeros((members, count), jnp.float32)
        for i, l in enumerate(levels):
            both = picked[2 * i * members : (2 * i + 1) * members] + picked[(2 * i + 1) * members : (2 * i + 2) * members]
            total = jnp.where(rows == l, both, total)
        for k in range(blocks):
            part[pl.ds((b * blocks + k) * members, members), :] = total[:, k * LANES : (k + 1) * LANES]
        copy = remote(part.at[pl.ds(start_of(b, (1 - core, half)), half)], in_core.at[b], core_sem.at[b, 0], core_sem.at[b, 1], pair)
        copy.start()
        core_out[b].append(copy)

    for b in every:
        core_out[b][0].wait_recv()
        part[pl.ds(start_of(b, (core, half)), half), :] += in_core[b]
        for j in range(1, plane_n):
            to = (spot + j) % plane_n
            copy = remote(
                part.at[pl.ds(start_of(b, (core, half), (to, size)), size)], in_plane.at[b, j - 1],
                plane_send.at[b, j - 1], plane_recv.at[b, j - 1], plane_at(to),
            )
            copy.start()
            plane_out[b].append(copy)
    for b in every:
        base = start_of(b, (core, half), (spot, size))
        total = part[pl.ds(base, size), :]
        for j in range(1, plane_n):
            plane_out[b][j - 1].wait_recv()
            total = total + in_plane[b, j - 1]
        part[pl.ds(base, size), :] = total
        for j in range(1, line_n):
            to = (line + j) % line_n
            start = start_of(b, (core, half), (spot, size), (to, piece)) if scatter else base
            copy = remote(part.at[pl.ds(start, piece)], in_line.at[b, j - 1], line_send.at[b, j - 1], line_recv.at[b, j - 1], line_at(to))
            copy.start()
            line_out[b].append(copy)
    for sends, receives, copy, _ in large:
        pl.when(sends)(copy.start)

    def spread_plane(b):
        view = prior.at[pl.ds(start_of(b, (core, half), (spot, size)), size)]
        for j in range(1, plane_n):
            k = plane_n - 1 + j - 1
            copy = remote(view, view, plane_send.at[b, k], plane_recv.at[b, k], plane_at((spot + j) % plane_n))
            copy.start()
            plane_back[b].append(copy)

    for b in every:
        own = start_of(b, (core, half), (spot, size), (line, piece)) if scatter else start_of(b, (core, half), (spot, size))
        total = part[pl.ds(own, piece), :]
        for j in range(1, line_n):
            line_out[b][j - 1].wait_recv()
            total = total + in_line[b, j - 1]
        prior[pl.ds(own, piece), :] = total
        if scatter:
            view = prior.at[pl.ds(own, piece)]
            for j in range(1, line_n):
                k = line_n - 1 + j - 1
                copy = remote(view, view, line_send.at[b, k], line_recv.at[b, k], line_at((line + j) % line_n))
                copy.start()
                line_back[b].append(copy)
        else:
            spread_plane(b)
    if scatter:
        for b in every:
            for copy in line_back[b]:
                copy.wait_recv()
            spread_plane(b)

    for sends, receives, copy, _ in large:
        pl.when(receives)(copy.wait_recv)
    state[0] += halo_u[...] * (diff_z[0:1, :] + 0.5 * cour_z[0:1, :])
    state[depth - 1] += halo_d[...] * (diff_z[depth - 1 : depth, :] - 0.5 * cour_z[depth - 1 : depth, :])
    keep = pltpu.make_async_copy(state, state_out, state_sem)
    keep.start()

    for b in every:
        for copy in plane_back[b]:
            copy.wait_recv()
        view = prior.at[pl.ds(start_of(b, (core, half)), half)]
        copy = remote(view, view, core_sem.at[b, 2], core_sem.at[b, 3], pair)
        copy.start()
        core_back[b].append(copy)
    for b in every:
        core_back[b][0].wait_recv()
    for group in (core_out, plane_out, line_out, line_back, plane_back, core_back):
        for copies in group:
            for copy in copies:
                copy.wait_send()
    for sends, receives, copy, _ in small + large:
        pl.when(sends)(copy.wait_send)
    keep.wait()


def update_kernel(
    total_cols, width, state_in, prior_in, cell_in, radius_in, value_in, var_in, out,
    layers_ref, later_ref, prior, obs_cell, obs_radius, obs_value, obs_var, load_sem,
):
    loads = []
    for i, (src, dst) in enumerate(
        (
            (cell_in, obs_cell), (radius_in, obs_radius), (value_in, obs_value), (var_in, obs_var),
            (prior_in, prior), (state_in, layers_ref),
        )
    ):
        copy = pltpu.make_async_copy(src, dst, load_sem.at[i])
        copy.start()
        loads.append(copy)
    depth, members, _ = layers_ref.shape
    batches, count = obs_cell.shape
    blocks = count // LANES
    first = lax.axis_index("tile") * width
    for copy in loads[:-1]:
        copy.wait()
    for b in range(batches):
        for k in range(blocks):
            later_ref[b, :, k * LANES : (k + 1) * LANES] = prior[pl.ds((b * blocks + k) * members, members), :]
    centre = split_cell(obs_cell[...], total_cols)[1].astype(jnp.float32)
    inverse = 1.0 / obs_radius[...].astype(jnp.float32)
    upright = jnp.concatenate([centre, inverse], axis=0).T
    grid = (first + lax.broadcasted_iota(jnp.int32, (1, width), 1)).astype(jnp.float32)

    for b in range(batches):
        y = later_ref[b]
        value, variance = obs_value[b : b + 1, :], obs_var[b : b + 1, :]
        ymean = jnp.sum(y, axis=0, keepdims=True) * (1.0 / members)
        anomaly = y - ymean
        spread = jnp.sum(anomaly * anomaly, axis=0, keepdims=True) / (members - 1) + 1e-06
        shrink = variance / (spread + variance)
        postmean = spread * shrink * (ymean / spread + value / variance)
        delta = (postmean - ymean) + (jnp.sqrt(shrink) - 1.0) * anomaly
        delta = delta * (1.0 / ((members - 1) * spread))
        d_high, d_low = halves(delta)
        d_both = jnp.concatenate([d_high, d_low], axis=0)
        y_high = anomaly.astype(jnp.bfloat16).astype(jnp.float32)
        y_low = anomaly - y_high
        lhs = jnp.concatenate([y_high, y_high, y_low, y_low], axis=0).T.astype(jnp.bfloat16)
        here, scale = upright[:, b : b + 1], upright[:, batches + b : batches + b + 1]

        def taper(positions):
            frac = jnp.maximum(1.0 - jnp.abs(positions - here) * scale, 0.0)
            return frac * frac

        def change(x, weight):
            x_high, x_low = halves(x - jnp.sum(x, axis=0, keepdims=True) * (1.0 / members))
            rhs = jnp.concatenate([x_high, x_low, x_high, x_low], axis=0)
            gain = jnp.dot(lhs, rhs, preferred_element_type=jnp.float32) * weight
            g_high, g_low = halves(gain)
            one = jnp.dot(d_both, g_high, preferred_element_type=jnp.float32)
            two = jnp.dot(d_high, g_low, preferred_element_type=jnp.float32)
            return one[:members] + one[members:] + two

        for c in range(b + 1, batches):
            later_ref[c] += change(later_ref[c], taper(centre[c : c + 1, :]))
        weight = taper(grid)
        if b == 0:
            loads[-1].wait()
        for l in range(depth):
            x = layers_ref[l]
            x = x + change(x, weight)
            if b == batches - 1:
                out[:, l, :] = x
            else:
                layers_ref[l] = x


def shards(ensemble, diff_x, diff_z, cour_x, cour_z, obs_cell, obs_radius, obs_value, obs_var):
    members, depth, width = ensemble.shape
    batches, count = obs_cell.shape
    tiles, layers = lax.axis_size("tile"), lax.axis_size("layer")
    rows = batches * count * members // LANES
    plane_n, line_n = layers * 2, tiles // 4
    half = rows // batches // 2
    size = half // plane_n
    piece = size // line_n if size % (8 * line_n) == 0 else size
    vmem = pl.BlockSpec(memory_space=pltpu.VMEM)
    hbm = pl.BlockSpec(memory_space=pltpu.HBM)
    f32 = jnp.float32
    dma = pltpu.SemaphoreType.DMA
    state, prior = pl.pallas_call(
        functools.partial(gather_kernel, tiles, layers),
        out_shape=(jax.ShapeDtypeStruct((depth, members, width), f32), jax.ShapeDtypeStruct((rows, LANES), f32)),
        in_specs=[hbm] * 6,
        out_specs=(hbm, vmem),
        scratch_shapes=[
            pltpu.VMEM((depth, members, width), f32),
            dma,
            pltpu.VMEM((members, depth, width), f32),
            *[pltpu.VMEM((depth, width), f32)] * 4,
            pltpu.VMEM((batches, count), jnp.int32),
            dma((6,)),
            pltpu.VMEM((depth, members, width), f32),
            *[pltpu.VMEM((members, LANES), f32)] * 4,
            *[pltpu.VMEM((members, width), f32)] * 2,
            *[pltpu.VMEM((8, width), f32)] * 4,
            pltpu.VMEM((rows, LANES), f32),
            pltpu.VMEM((batches, half, LANES), f32),
            pltpu.VMEM((batches, plane_n - 1, size, LANES), f32),
            pltpu.VMEM((batches, line_n - 1, piece, LANES), f32),
            dma((6,)),
            dma((6,)),
            dma((batches, 4)),
            dma((batches, 2 * plane_n - 2)),
            dma((batches, 2 * plane_n - 2)),
            dma((batches, 2 * line_n - 2)),
            dma((batches, 2 * line_n - 2)),
        ],
        compiler_params=pltpu.CompilerParams(collective_id=0, has_side_effects=True, vmem_limit_bytes=63 * 2**20),
        name="gather_prior",
    )(ensemble, diff_x, diff_z, cour_x, cour_z, obs_cell)
    return pl.pallas_call(
        functools.partial(update_kernel, tiles * width, width),
        out_shape=jax.ShapeDtypeStruct((members, depth, width), f32),
        in_specs=[hbm] * 6,
        out_specs=vmem,
        scratch_shapes=[
            pltpu.VMEM((depth, members, width), f32),
            pltpu.VMEM((batches, members, count), f32),
            pltpu.VMEM((rows, LANES), f32),
            *[pltpu.VMEM((batches, count), jnp.int32)] * 2,
            *[pltpu.VMEM((batches, count), f32)] * 2,
            dma((6,)),
        ],
        compiler_params=pltpu.CompilerParams(vmem_limit_bytes=63 * 2**20),
        name="update",
    )(state, prior, obs_cell, obs_radius, obs_value, obs_var)


def solution(mesh):
    in_specs = (
        P(None, "layer", "tile"),
        P("layer", "tile"),
        P("layer", "tile"),
        P("layer", "tile"),
        P("layer", "tile"),
        P(),
        P(),
        P(),
        P(),
    )
    out_specs = P(None, "layer", "tile")
    return jax.shard_map(shards, mesh=mesh, in_specs=in_specs, out_specs=out_specs, check_vma=False)
```

profile of v0, /device:TPU:1, one launch (start us, length us, event | category | flops | bytes accessed | tf_op | source)
XLA Modules:
  0.0 42.5 jit_solution(9981923671193935625)
XLA Ops:
  0.0 29.5 %gather_prior.1 = (f32[4,64,512]{2,1,0:T(8,128)}, f32[1024,128]{1,0:T(8,128)}) custom-call(f32[64,4,512]{2,1,0:T(4,128)} %ens_in.1, f32[4,512]{1,0:T(4,128)} %dx_in.1, f32[4,512]{1,0:T(4,128)} %dz_in.1, f32[4,512]{1,0:T(4,128)} %cx_in.1, f32[4,512]{1,0:T(4,128)} %cz_in.1, s32[4,512]{1,0:T(4,128)} %cell_in.3), custom_call_target="tpu_custom_call" | custom-call | tf_op jit(solution)/shard_map/gather_prior/pallas_call | solution.py:329
  29.6 13.0 %update.1 = f32[64,4,512]{2,1,0:T(4,128)} custom-call(f32[4,64,512]{2,1,0:T(8,128)} %get-tuple-element.7.state_in, f32[1024,128]{1,0:T(8,128)} %get-tuple-element.8.prior_in, s32[4,512]{1,0:T(4,128)} %cell_in.3, s32[4,512]{1,0:T(4,128)} %radius_in.1, f32[4,512]{1,0:T(4,128)} %value_in.1, f32[4,512]{1,0:T(4,128)} %var_in.1), custom_call_target="tpu_custom_call" | custom-call | tf_op jit(solution)/shard_map/update/pallas_call | solution.py:360
where the time goes:
time: 42.8 us; the launch traced here: 42.5 us
  Pallas kernels  42.5 us (99%)
    pallas_call x1, Pallas kernels, shards(): pl.pallas_call(functools.partial(gather_kernel, tiles, layers), out_shape...  29.5 us
    pallas_call x1, Pallas kernels, shards(): pl.pallas_call(functools.partial(update_kernel, tiles * width, width), ou...  13 us

commit v1 on v0

--- a/solution.py
+++ b/solution.py
@@ -313,7 +313,375 @@
                 layers_ref[l] = x
 
 
-def shards(ensemble, diff_x, diff_z, cour_x, cour_z, obs_cell, obs_radius, obs_value, obs_var):
+def divide(values, size):
+    return values >> (size.bit_length() - 1) if size & (size - 1) == 0 else values // size
+
+
+def dot_rows(a, b):
+    return lax.dot_general(a, b, (((1,), (1,)), ((), ())), preferred_element_type=jnp.float32)
+
+
+def remote(src, dst, send, recv, device):
+    return pltpu.make_async_remote_copy(
+        src_ref=src, dst_ref=dst, send_sem=send, recv_sem=recv, device_id=device, device_id_type=MESH
+    )
+
+
+def collect_kernel(
+    tiles, layers, cap, ens_in, dx_in, dz_in, cx_in, cz_in, cell_in, radius_in, value_in, var_in,
+    state_out, gathered, meta, table, flag,
+    state, state_sem, ens, diff_x, diff_z, cour_x, cour_z, obs_cell, obs_radius, obs_value, obs_var, load_sem,
+    cells, edge_w, edge_e, halo_w, halo_e, near_u, near_d, part_u, part_d, halo_u, halo_d,
+    hop_send, hop_recv, line_send, line_recv, plane_send, plane_recv, core_send, core_recv,
+):
+    loads = []
+    for i, (src, dst) in enumerate(
+        (
+            (cell_in, obs_cell), (ens_in, ens), (dz_in, diff_z), (cz_in, cour_z), (dx_in, diff_x), (cx_in, cour_x),
+            (radius_in, obs_radius), (value_in, obs_value), (var_in, obs_var),
+        )
+    ):
+        copy = pltpu.make_async_copy(src, dst, load_sem.at[i])
+        copy.start()
+        loads.append(copy)
+    members, depth, width = ens.shape
+    batches, count = obs_cell.shape
+    chunks, devices, piece, _ = gathered.shape
+    f32, bf16 = jnp.float32, jnp.bfloat16
+    tile, layer = lax.axis_index("tile"), lax.axis_index("layer")
+    core, row, line = tile % 2, (tile // 2) % 2, tile // 4
+    plane_n, line_n = layers * 2, tiles // 4
+    spot = layer * 2 + row
+    pair = (tile + 1 - 2 * core, layer)
+
+    def plane_at(index):
+        return (line * 4 + (index % 2) * 2 + core, index // 2)
+
+    def line_at(index):
+        return (index * 4 + row * 2 + core, layer)
+
+    above, below = (tile, lax.rem(layer + layers - 1, layers)), (tile, lax.rem(layer + 1, layers))
+    ahead, behind = (lax.rem(tile + 1, tiles), layer), (lax.rem(tile + tiles - 1, tiles), layer)
+    greeted = [pair, ahead, behind, below, above]
+    greeted += [plane_at((spot + j) % plane_n) for j in range(1, plane_n)]
+    greeted += [line_at((line + j) % line_n) for j in range(1, line_n)]
+    barrier = pltpu.get_barrier_semaphore()
+    for device in greeted:
+        pl.semaphore_signal(barrier, inc=1, device_id=device, device_id_type=MESH)
+
+    loads[0].wait()
+    cell_row, cell_col = split_cell(obs_cell[...], tiles * width)
+    cell_tile, cell_layer = divide(cell_col, width), divide(cell_row, depth)
+    local_col, local_row = cell_col - cell_tile * width, cell_row - cell_layer * depth
+    here = cell_tile == tile
+    groups = [
+        jnp.where(jnp.logical_and(here, cell_layer == layer + step), 1.0, 0.0) for step in (0, -1, 1)
+    ]
+    masks = jnp.concatenate(groups + [jnp.zeros_like(groups[0])], axis=0).astype(bf16)
+    first = lax.broadcasted_iota(jnp.int32, (count, count), 0)
+    second = lax.broadcasted_iota(jnp.int32, (count, count), 1)
+    running = jnp.dot(masks, jnp.where(first <= second, 1.0, 0.0).astype(bf16), preferred_element_type=f32)
+    code = (local_row * width + local_col + 1).astype(f32)
+    slot = lax.broadcasted_iota(jnp.int32, (cap, count), 0).astype(f32)
+    lane_w = lax.broadcasted_iota(jnp.int32, (cap, width), 1)
+    found = []
+    for k, edge in enumerate((None, depth - 1, 0)):
+        before_ = jnp.zeros((1, 1), f32)
+        total = jnp.zeros((cap, count), f32)
+        for b in range(batches):
+            i = k * batches + b
+            wanted = groups[k][b : b + 1, :] > 0.5
+            if edge is not None:
+                wanted = jnp.logical_and(wanted, local_row[b : b + 1, :] == edge)
+            rank = jnp.where(wanted, running[i : i + 1, :] + (before_ - 1.0), -1.0)
+            total = total + jnp.where(rank == slot, code[b : b + 1, :], 0.0)
+            before_ = before_ + running[i : i + 1, count - 1 : count]
+        cell = jnp.sum(total, axis=1, keepdims=True).astype(jnp.int32) - 1
+        at_row = divide(cell, width)
+        at_col = jnp.where(cell >= 0, cell - at_row * width, -1)
+        found.append((at_row, at_col, jnp.where(lane_w == at_col, 1.0, 0.0)))
+
+    low = lax.broadcasted_iota(jnp.int32, (piece, LANES), 1) < members
+
+    def packed(values):
+        out = []
+        for k in range(chunks):
+            base = 2 * piece * k
+            out.append(jnp.where(low, values[base : base + piece], values[base + piece : base + 2 * piece]))
+        return out
+
+    def doubled(values):
+        return values + pltpu.roll(values, members, 1)
+
+    for copy in loads[1:6]:
+        copy.wait()
+    lane = lax.broadcasted_iota(jnp.int32, (members, LANES), 1)
+    west = jnp.zeros((members, LANES), f32)
+    east = jnp.zeros((members, LANES), f32)
+    for l in range(depth):
+        x = ens[:, l, :]
+        cells[l] = x
+        west = jnp.where(lane == l, x[:, 0:1], west)
+        east = jnp.where(lane == l, x[:, width - 1 : width], east)
+    edge_w[...] = jnp.concatenate([west, west], axis=0).T[:8]
+    edge_e[...] = jnp.concatenate([east, east], axis=0).T[:8]
+    for ref, k, l in ((part_u, 1, 0), (part_d, 2, depth - 1)):
+        raw = jnp.concatenate(halves(cells[l]), axis=0)
+        for i, rows in enumerate(packed(doubled(dot_rows(found[k][2].astype(bf16), raw)))):
+            ref[i * piece : (i + 1) * piece, :] = rows
+    pl.semaphore_wait(barrier, len(greeted))
+
+    up, down = layer > 0, layer < layers - 1
+    before, after = tile > 0, tile < tiles - 1
+
+    def move(i, sends, receives, src, dst, device):
+        return sends, receives, remote(src, dst, hop_send.at[i], hop_recv.at[i], device), dst
+
+    small = (
+        move(0, down, up, part_d, near_u, below),
+        move(1, up, down, part_u, near_d, above),
+        move(2, after, before, edge_e, halo_w, ahead),
+        move(3, before, after, edge_w, halo_e, behind),
+    )
+    large = (
+        move(4, down, up, cells.at[depth - 1], halo_u, below),
+        move(5, up, down, cells.at[0], halo_d, above),
+    )
+    for sends, receives, copy, place in small:
+        pl.when(sends)(copy.start)
+    for sends, receives, copy, place in small + large:
+
+        @pl.when(jnp.logical_not(receives))
+        def _(place=place):
+            place[...] = jnp.zeros_like(place)
+
+    at_row, at_col, hot = found[0]
+    column = lax.broadcasted_iota(jnp.int32, (members, width), 1)
+    total = jnp.zeros((cap, LANES), f32)
+    for l in range(depth):
+        x = cells[l]
+        left = jnp.where(column == 0, 0.0, pltpu.roll(x, 1, 1))
+        right = jnp.where(column == width - 1, 0.0, pltpu.roll(x, width - 1, 1))
+        dx, dz = diff_x[l : l + 1, :], diff_z[l : l + 1, :]
+        cx, cz = 0.5 * cour_x[l : l + 1, :], 0.5 * cour_z[l : l + 1, :]
+        new = x * (1.0 - 2.0 * dz - 2.0 * dx) + left * (dx + cx) + right * (dx - cx)
+        if l > 0:
+            new = new + cells[l - 1] * (dz + cz)
+        if l < depth - 1:
+            new = new + cells[l + 1] * (dz - cz)
+        state[l] = new
+        picked = dot_rows(hot.astype(bf16), jnp.concatenate(halves(new), axis=0))
+        total = total + jnp.where(at_row == l, picked, 0.0)
+    mine = packed(doubled(total))
+    coef_u = diff_z[0:1, :] + 0.5 * cour_z[0:1, :]
+    coef_d = diff_z[depth - 1 : depth, :] - 0.5 * cour_z[depth - 1 : depth, :]
+    take_u = jnp.where(at_row == 0, jnp.sum(hot * coef_u, axis=1, keepdims=True), 0.0)
+    take_d = jnp.where(at_row == depth - 1, jnp.sum(hot * coef_d, axis=1, keepdims=True), 0.0)
+    coef_w = diff_x[:, 0:1] + 0.5 * cour_x[:, 0:1]
+    coef_e = diff_x[:, width - 1 : width] - 0.5 * cour_x[:, width - 1 : width]
+    weights = [packed(jnp.broadcast_to(take, (cap, LANES))) for take in (take_u, take_d)]
+    sides = []
+    for at, coef in ((0, coef_w), (width - 1, coef_e)):
+        for l in range(depth):
+            take = jnp.where(jnp.logical_and(at_row == l, at_col == at), coef[l : l + 1, :], 0.0)
+            sides.append(packed(jnp.broadcast_to(take, (cap, LANES))))
+
+    for sends, receives, copy, place in small:
+        pl.when(receives)(copy.wait_recv)
+    me = (core * plane_n + spot) * line_n + line
+    line_out, plane_out, core_out = ([[] for _ in range(chunks)] for _ in range(3))
+    for k in range(chunks):
+        rows = pl.ds(k * piece, piece)
+        value = mine[k] + weights[0][k] * near_u[rows, :] + weights[1][k] * near_d[rows, :]
+        for l in range(depth):
+            value = value + sides[l][k] * halo_w[l : l + 1, :] + sides[depth + l][k] * halo_e[l : l + 1, :]
+        gathered[k, me] = value
+        view = gathered.at[k, me]
+        for j in range(1, line_n):
+            copy = remote(view, view, line_send.at[k, j - 1], line_recv.at[k, j - 1], line_at((line + j) % line_n))
+            copy.start()
+            line_out[k].append(copy)
+    for sends, receives, copy, _ in large:
+        pl.when(sends)(copy.start)
+
+    for ref, coef, at in ((halo_w, coef_w, 0), (halo_e, coef_e, width - 1)):
+        base = at // LANES * LANES
+        block = lax.broadcasted_iota(jnp.int32, (members, LANES), 1)
+        turned = jnp.concatenate([ref[...]] * (LANES // 8), axis=0).T[:members]
+        for l in range(depth):
+            term = turned[:, l : l + 1] * coef[l : l + 1, :]
+            state[l, :, base : base + LANES] += jnp.where(block == at - base, term, 0.0)
+
+    for copy in loads[6:]:
+        copy.wait()
+    core_of, row_of, line_of = cell_tile & 1, divide(cell_tile, 2) & 1, divide(cell_tile, 4)
+    owner = (core_of * plane_n + cell_layer * 2 + row_of) * line_n + line_of
+    key = (owner * count + lax.broadcasted_iota(jnp.int32, (batches, count), 1)).astype(f32)
+    both = jnp.concatenate([key, owner.astype(f32)], axis=0)
+    if 2 * batches % 8:
+        both = jnp.concatenate([both, jnp.zeros((8 - 2 * batches % 8, count), f32)], axis=0)
+    upright = both.T
+
+    def pieces(values, n):
+        out = []
+        for _ in range(n):
+            high = values.astype(bf16).astype(f32)
+            out.append(high)
+            values = values - high
+        return out
+
+    fields = (
+        (cell_col.astype(f32), 2), (obs_radius[...].astype(f32), 2), (obs_value[...], 3), (obs_var[...], 3)
+    )
+    parts = []
+    for values, n in fields:
+        parts.extend(pieces(values, n))
+    wide = table.shape[1]
+    lane_d = lax.broadcasted_iota(jnp.int32, (count, wide), 1).astype(f32)
+    used = jnp.zeros((1, wide), f32)
+    if len(parts) * batches % 16:
+        parts.append(jnp.zeros((16 - len(parts) * batches % 16, count), f32))
+    parts = jnp.concatenate(parts, axis=0).astype(bf16)
+    place = first.astype(f32)
+    for b in range(batches):
+        less = jnp.where(upright[:, b : b + 1] < key[b : b + 1, :], 1.0, 0.0)
+        position = jnp.sum(less, axis=0, keepdims=True)
+        order = jnp.where(place == position, 1.0, 0.0).astype(bf16)
+        ordered = dot_rows(parts, order)
+        i = 0
+        for f, (_, n) in enumerate(fields):
+            total = ordered[i * batches + b : i * batches + b + 1, :]
+            for p in range(1, n):
+                total = total + ordered[(i + p) * batches + b : (i + p) * batches + b + 1, :]
+            meta[f * batches + b : f * batches + b + 1, :] = total
+            i += n
+        holder = upright[:, batches + b : batches + b + 1]
+        length = jnp.sum(jnp.where(holder == lane_d, 1.0, 0.0), axis=0, keepdims=True)
+        start = jnp.sum(jnp.where(holder < lane_d, 1.0, 0.0), axis=0, keepdims=True)
+        table[b : b + 1, :] = length.astype(jnp.int32)
+        table[batches + b : batches + b + 1, :] = start.astype(jnp.int32)
+        table[2 * batches + b : 2 * batches + b + 1, :] = used.astype(jnp.int32)
+        used = used + length
+    flag[0] = (jnp.max(used) > cap).astype(jnp.int32)
+
+    for k in range(chunks):
+        for copy in line_out[k]:
+            copy.wait_recv()
+        view = gathered.at[k, pl.ds((core * plane_n + spot) * line_n, line_n)]
+        for j in range(1, plane_n):
+            copy = remote(view, view, plane_send.at[k, j - 1], plane_recv.at[k, j - 1], plane_at((spot + j) % plane_n))
+            copy.start()
+            plane_out[k].append(copy)
+
+    for sends, receives, copy, _ in large:
+        pl.when(receives)(copy.wait_recv)
+    state[0] += halo_u[...] * coef_u
+    state[depth - 1] += halo_d[...] * coef_d
+    keep = pltpu.make_async_copy(state, state_out, state_sem)
+    keep.start()
+
+    for k in range(chunks):
+        for copy in plane_out[k]:
+            copy.wait_recv()
+        view = gathered.at[k, pl.ds(core * plane_n * line_n, plane_n * line_n)]
+        copy = remote(view, view, core_send.at[k], core_recv.at[k], pair)
+        copy.start()
+        core_out[k].append(copy)
+    for k in range(chunks):
+        core_out[k][0].wait_recv()
+    for group in (line_out, plane_out, core_out):
+        for copies in group:
+            for copy in copies:
+                copy.wait_send()
+    for sends, receives, copy, _ in small + large:
+        pl.when(sends)(copy.wait_send)
+    keep.wait()
+
+
+def apply_kernel(
+    cap, width, table, state_in, gathered, meta, out, layers_ref, later_ref, flat, ordered, load_sem,
+):
+    load = pltpu.make_async_copy(state_in, layers_ref, load_sem)
+    load.start()
+    depth, members, _ = layers_ref.shape
+    batches, _, count = later_ref.shape
+    chunks, devices, piece, _ = gathered.shape
+    first = lax.axis_index("tile") * width
+    for k in range(chunks):
+        for g in range(devices):
+            rows = gathered[k, g]
+            at = g * cap + 2 * piece * k
+            flat[at : at + piece, :] = rows
+            flat[at + piece : at + 2 * piece, :] = pltpu.roll(rows, members, 1)
+
+    run = min(cap, (count // devices + 7) // 8 * 8 + 8)
+
+    def spread(g, carry):
+        for b in range(batches):
+            dst, src = table[batches + b, g], g * cap + table[2 * batches + b, g]
+            for i in range(0, run, 8):
+                ordered[b, pl.ds(dst + i, 8), :] = flat[pl.ds(src + i, 8), :]
+
+            @pl.when(table[b, g] > run)
+            def _(b=b, dst=dst, src=src):
+                for i in range(run, cap, 8):
+                    ordered[b, pl.ds(dst + i, 8), :] = flat[pl.ds(src + i, 8), :]
+
+        return carry
+
+    lax.fori_loop(0, devices, spread, 0)
+    for b in range(batches):
+        later_ref[b] = ordered[b, :count, :].T[:members]
+    centre = meta[0:batches, :]
+    inverse = 1.0 / meta[batches : 2 * batches, :]
+    upright = jnp.concatenate([centre, inverse], axis=0).T
+    grid = (first + lax.broadcasted_iota(jnp.int32, (1, width), 1)).astype(jnp.float32)
+
+    for b in range(batches):
+        y = later_ref[b]
+        value, variance = meta[2 * batches + b : 2 * batches + b + 1, :], meta[3 * batches + b : 3 * batches + b + 1, :]
+        ymean = jnp.sum(y, axis=0, keepdims=True) * (1.0 / members)
+        anomaly = y - ymean
+        spread = jnp.sum(anomaly * anomaly, axis=0, keepdims=True) / (members - 1) + 1e-06
+        shrink = variance / (spread + variance)
+        postmean = spread * shrink * (ymean / spread + value / variance)
+        delta = (postmean - ymean) + (jnp.sqrt(shrink) - 1.0) * anomaly
+        delta = delta * (1.0 / ((members - 1) * spread))
+        d_high, d_low = halves(delta)
+        d_both = jnp.concatenate([d_high, d_low], axis=0)
+        y_high = anomaly.astype(jnp.bfloat16).astype(jnp.float32)
+        y_low = anomaly - y_high
+        lhs = jnp.concatenate([y_high, y_high, y_low, y_low], axis=0).T.astype(jnp.bfloat16)
+        here, scale = upright[:, b : b + 1], upright[:, batches + b : batches + b + 1]
+
+        def taper(positions):
+            frac = jnp.maximum(1.0 - jnp.abs(positions - here) * scale, 0.0)
+            return frac * frac
+
+        def change(x, weight):
+            x_high, x_low = halves(x - jnp.sum(x, axis=0, keepdims=True) * (1.0 / members))
+            rhs = jnp.concatenate([x_high, x_low, x_high, x_low], axis=0)
+            gain = jnp.dot(lhs, rhs, preferred_element_type=jnp.float32) * weight
+            g_high, g_low = halves(gain)
+            one = jnp.dot(d_both, g_high, preferred_element_type=jnp.float32)
+            two = jnp.dot(d_high, g_low, preferred_element_type=jnp.float32)
+            return one[:members] + one[members:] + two
+
+        for c in range(b + 1, batches):
+            later_ref[c] += change(later_ref[c], taper(centre[c : c + 1, :]))
+        weight = taper(grid)
+        if b == 0:
+            load.wait()
+        for l in range(depth):
+            x = layers_ref[l]
+            x = x + change(x, weight)
+            if b == batches - 1:
+                out[:, l, :] = x
+            else:
+                layers_ref[l] = x
+
+
+def slow_shards(ensemble, diff_x, diff_z, cour_x, cour_z, obs_cell, obs_radius, obs_value, obs_var):
     members, depth, width = ensemble.shape
     batches, count = obs_cell.shape
     tiles, layers = lax.axis_size("tile"), lax.axis_size("layer")
@@ -375,6 +743,78 @@
     )(state, prior, obs_cell, obs_radius, obs_value, obs_var)
 
 
+def shards(ensemble, diff_x, diff_z, cour_x, cour_z, obs_cell, obs_radius, obs_value, obs_var):
+    members, depth, width = ensemble.shape
+    batches, count = obs_cell.shape
+    tiles, layers = lax.axis_size("tile"), lax.axis_size("layer")
+    devices = tiles * layers
+    plane_n, line_n = layers * 2, tiles // 4
+    mean = batches * count / devices
+    cap = -int(-(mean + 4.0 * mean**0.5) // 16) * 16
+    piece = 16 if cap % 32 == 0 else 8
+    chunks = cap // (2 * piece)
+    wide = -(-devices // LANES) * LANES
+    vmem = pl.BlockSpec(memory_space=pltpu.VMEM)
+    smem = pl.BlockSpec(memory_space=pltpu.SMEM)
+    hbm = pl.BlockSpec(memory_space=pltpu.HBM)
+    f32 = jnp.float32
+    dma = pltpu.SemaphoreType.DMA
+    state, gathered, meta, table, flag = pl.pallas_call(
+        functools.partial(collect_kernel, tiles, layers, cap),
+        out_shape=(
+            jax.ShapeDtypeStruct((depth, members, width), f32),
+            jax.ShapeDtypeStruct((chunks, devices, piece, LANES), f32),
+            jax.ShapeDtypeStruct((4 * batches, count), f32),
+            jax.ShapeDtypeStruct((3 * batches, wide), jnp.int32),
+            jax.ShapeDtypeStruct((1,), jnp.int32),
+        ),
+        in_specs=[hbm] * 9,
+        out_specs=(hbm, vmem, vmem, vmem, smem),
+        scratch_shapes=[
+            pltpu.VMEM((depth, members, width), f32),
+            dma,
+            pltpu.VMEM((members, depth, width), f32),
+            *[pltpu.VMEM((depth, width), f32)] * 4,
+            *[pltpu.VMEM((batches, count), jnp.int32)] * 2,
+            *[pltpu.VMEM((batches, count), f32)] * 2,
+            dma((9,)),
+            pltpu.VMEM((depth, members, width), f32),
+            *[pltpu.VMEM((8, LANES), f32)] * 4,
+            *[pltpu.VMEM((cap // 2, LANES), f32)] * 4,
+            *[pltpu.VMEM((members, width), f32)] * 2,
+            dma((6,)),
+            dma((6,)),
+            *[dma((chunks, max(line_n - 1, 1)))] * 2,
+            *[dma((chunks, plane_n - 1))] * 2,
+            *[dma((chunks,))] * 2,
+        ],
+        compiler_params=pltpu.CompilerParams(collective_id=1, has_side_effects=True, vmem_limit_bytes=48 * 2**20),
+        name="collect",
+    )(ensemble, diff_x, diff_z, cour_x, cour_z, obs_cell, obs_radius, obs_value, obs_var)
+
+    def fast():
+        return pl.pallas_call(
+            functools.partial(apply_kernel, cap, width),
+            out_shape=jax.ShapeDtypeStruct((members, depth, width), f32),
+            in_specs=[smem, hbm, vmem, vmem],
+            out_specs=vmem,
+            scratch_shapes=[
+                pltpu.VMEM((depth, members, width), f32),
+                pltpu.VMEM((batches, members, count), f32),
+                pltpu.VMEM((devices * cap + cap, LANES), f32),
+                pltpu.VMEM((batches, count + cap, LANES), f32),
+                dma,
+            ],
+            compiler_params=pltpu.CompilerParams(vmem_limit_bytes=48 * 2**20),
+            name="apply",
+        )(table, state, gathered, meta)
+
+    def slow():
+        return slow_shards(ensemble, diff_x, diff_z, cour_x, cour_z, obs_cell, obs_radius, obs_value, obs_var)
+
+    return lax.cond(flag[0] > 0, slow, fast)
+
+
 def solution(mesh):
     in_specs = (
         P(None, "layer", "tile"),

time: 42.8 us -> 35.4 us (0.83)
  Pallas kernels: 42.5 us -> 34 us
  between operations: 0.01 us -> 0.86 us
    pallas_call x2, Pallas kernels: 42.5 us -> 34 us  [the longest x1 19.6 us: shards(): pl.pallas_call(functools.partial(collect_kernel, tiles, layers, cap), out...]
where the time goes in v1:
time: 35.4 us; the launch traced here: 35.1 us
  Pallas kernels  34 us (96%)
  between operations  0.86 us (2%)
    pallas_call x1, Pallas kernels, shards(): pl.pallas_call(functools.partial(collect_kernel, tiles, layers, cap), out...  19.6 us
    pallas_call x1, Pallas kernels, fast(): pl.pallas_call(functools.partial(apply_kernel, cap, width), out_shape=jax...  14.4 us

profile of v1, /device:TPU:1, one launch (start us, length us, event | category | flops | bytes accessed | tf_op | source)
XLA Modules:
  0.0 35.1 jit_solution(5784534728930832693)
XLA Ops:
  0.0 0.0 copy-start
  0.0 0.0 copy-start.2
  0.0 0.0 copy-start.3
  0.0 0.0 copy-start.4
  0.0 0.0 copy-start.5
  0.0 0.0 copy-start.6
  0.0 0.0 copy-start.7
  0.0 0.0 copy-start.8
  0.1 19.6 %collect.1 = (f32[4,64,512]{2,1,0:T(8,128)S(1)}, f32[3,32,16,128]{3,2,1,0:T(8,128)S(1)}, f32[16,512]{1,0:T(8,128)S(1)}, s32[12,128]{1,0:T(8,128)S(1)}, s32[1]{0:T(128)}) custom-call(f32[64,4,512]{2,1,0:T(4,128)} %ens_in.1, f32[4,512]{1,0:T(4,128)} %dx_in.1, f32[4,512]{1,0:T(4,128)} %dz_in.1, f32[4,512]{1,0:T(4,128)} %cx_in.1, f32[4,512]{1,0:T(4,128)} %cz_in.1, ...), custom_call_target="tpu_custom_call" | custom-call | tf_op jit(solution)/shard_map/collect/pallas_call | solution.py:762
  19.7 0.0 copy-start.1
  20.2 0.0 copy-done
  20.3 0.0 copy-done.2
  20.3 0.0 copy-done.3
  20.3 0.0 copy-done.4
  20.3 0.0 copy-done.5
  20.3 0.0 copy-done.6
  20.3 0.0 copy-done.7
  20.3 0.0 copy-done.8
  20.3 0.0 copy-done.1
  20.4 14.6 %conditional.1 = (f32[64,4,512]{2,1,0:T(4,128)}) conditional(s32[]{:T(128)} %bitcast, (s32[12,128]{1,0:T(8,128)S(1)}, f32[4,64,512]{2,1,0:T(8,128)S(1)}, f32[3,32,16,128]{3,2,1,0:T(8,128)S(1)}, f32[16,512]{1,0:T(8,128)S(1)}) %tuple.11, (f32[64,4,512]{2,1,0:T(4,128)S(1)}, f32[4,512]{1,0:T(4,128)S(1)}, f32[4,512]{1,0:T(4,128)S(1)}, ...), branch_computations={%region_0.0_spmd, %region_1.0_spmd} | conditional | bytes 8 | solution.py:815
  20.5 14.4 %apply.1 = f32[64,4,512]{2,1,0:T(4,128)} custom-call(s32[12,128]{1,0:T(8,128)S(1)} %get-tuple-element.34.table, f32[4,64,512]{2,1,0:T(8,128)S(1)} %get-tuple-element.35.state_in, f32[3,32,16,128]{3,2,1,0:T(8,128)S(1)} %get-tuple-element.36.gathered, f32[16,512]{1,0:T(8,128)S(1)} %get-tuple-element.37.meta), custom_call_target="tpu_custom_call" | custom-call | tf_op jit(solution)/shard_map/cond/branch_0_fun/apply/pallas_call | solution.py:796
Async XLA Ops:
  0.0 20.2 %copy-start = (f32[64,4,512]{2,1,0:T(4,128)S(1)}, f32[64,4,512]{2,1,0:T(4,128)}, u32[]{:S(2)}) copy-start(f32[64,4,512]{2,1,0:T(4,128)} %ens_in.1) | copy-start | bytes 1572868
  0.0 20.3 %copy-start.2 = (f32[4,512]{1,0:T(4,128)S(1)}, f32[4,512]{1,0:T(4,128)}, u32[]{:S(2)}) copy-start(f32[4,512]{1,0:T(4,128)} %dx_in.1) | copy-start | bytes 24580
  0.0 20.3 %copy-start.3 = (f32[4,512]{1,0:T(4,128)S(1)}, f32[4,512]{1,0:T(4,128)}, u32[]{:S(2)}) copy-start(f32[4,512]{1,0:T(4,128)} %dz_in.1) | copy-start | bytes 24580
  0.0 20.3 %copy-start.4 = (f32[4,512]{1,0:T(4,128)S(1)}, f32[4,512]{1,0:T(4,128)}, u32[]{:S(2)}) copy-start(f32[4,512]{1,0:T(4,128)} %cx_in.1) | copy-start | bytes 24580
  0.0 20.3 %copy-start.5 = (f32[4,512]{1,0:T(4,128)S(1)}, f32[4,512]{1,0:T(4,128)}, u32[]{:S(2)}) copy-start(f32[4,512]{1,0:T(4,128)} %cz_in.1) | copy-start | bytes 24580
  0.0 20.3 %copy-start.6 = (s32[4,512]{1,0:T(4,128)S(1)}, s32[4,512]{1,0:T(4,128)}, u32[]{:S(2)}) copy-start(s32[4,512]{1,0:T(4,128)} %radius_in.1) | copy-start | bytes 24580
  0.0 20.3 %copy-start.7 = (f32[4,512]{1,0:T(4,128)S(1)}, f32[4,512]{1,0:T(4,128)}, u32[]{:S(2)}) copy-start(f32[4,512]{1,0:T(4,128)} %value_in.1) | copy-start | bytes 24580
  0.0 20.3 %copy-start.8 = (f32[4,512]{1,0:T(4,128)S(1)}, f32[4,512]{1,0:T(4,128)}, u32[]{:S(2)}) copy-start(f32[4,512]{1,0:T(4,128)} %var_in.1) | copy-start | bytes 24580
  19.7 0.7 %copy-start.1 = (s32[4,512]{1,0:T(4,128)S(1)}, s32[4,512]{1,0:T(4,128)}, u32[]{:S(2)}) copy-start(s32[4,512]{1,0:T(4,128)} %cell_in.1) | copy-start | bytes 24580

commit v2 on v1

--- a/solution.py
+++ b/solution.py
@@ -329,7 +329,7 @@
 
 def collect_kernel(
     tiles, layers, cap, ens_in, dx_in, dz_in, cx_in, cz_in, cell_in, radius_in, value_in, var_in,
-    state_out, gathered, meta, table, flag,
+    state_out, gathered, meta, taper_in, kinks, table, flag,
     state, state_sem, ens, diff_x, diff_z, cour_x, cour_z, obs_cell, obs_radius, obs_value, obs_var, load_sem,
     cells, edge_w, edge_e, halo_w, halo_e, near_u, near_d, part_u, part_d, halo_u, halo_d,
     hop_send, hop_recv, line_send, line_recv, plane_send, plane_recv, core_send, core_recv,
@@ -517,10 +517,7 @@
     core_of, row_of, line_of = cell_tile & 1, divide(cell_tile, 2) & 1, divide(cell_tile, 4)
     owner = (core_of * plane_n + cell_layer * 2 + row_of) * line_n + line_of
     key = (owner * count + lax.broadcasted_iota(jnp.int32, (batches, count), 1)).astype(f32)
-    both = jnp.concatenate([key, owner.astype(f32)], axis=0)
-    if 2 * batches % 8:
-        both = jnp.concatenate([both, jnp.zeros((8 - 2 * batches % 8, count), f32)], axis=0)
-    upright = both.T
+    upright = jnp.concatenate([key, jnp.zeros_like(key)], axis=0).T
 
     def pieces(values, n):
         out = []
@@ -536,9 +533,11 @@
     parts = []
     for values, n in fields:
         parts.extend(pieces(values, n))
-    wide = table.shape[1]
-    lane_d = lax.broadcasted_iota(jnp.int32, (count, wide), 1).astype(f32)
-    used = jnp.zeros((1, wide), f32)
+    devices_at = lax.broadcasted_iota(jnp.int32, (devices, count), 0)
+    tiles_at = lax.broadcasted_iota(jnp.int32, (tiles, count), 0)
+    ends = [divide(cell_col + obs_radius[...] * step, width) for step in (-1, 0, 1)]
+    used = jnp.zeros((devices, 1), f32)
+    worst = jnp.zeros((tiles, 1), f32)
     if len(parts) * batches % 16:
         parts.append(jnp.zeros((16 - len(parts) * batches % 16, count), f32))
     parts = jnp.concatenate(parts, axis=0).astype(bf16)
@@ -555,14 +554,19 @@
                 total = total + ordered[(i + p) * batches + b : (i + p) * batches + b + 1, :]
             meta[f * batches + b : f * batches + b + 1, :] = total
             i += n
-        holder = upright[:, batches + b : batches + b + 1]
-        length = jnp.sum(jnp.where(holder == lane_d, 1.0, 0.0), axis=0, keepdims=True)
-        start = jnp.sum(jnp.where(holder < lane_d, 1.0, 0.0), axis=0, keepdims=True)
-        table[b : b + 1, :] = length.astype(jnp.int32)
-        table[batches + b : batches + b + 1, :] = start.astype(jnp.int32)
-        table[2 * batches + b : 2 * batches + b + 1, :] = used.astype(jnp.int32)
+        holder = owner[b : b + 1, :]
+        length = jnp.sum(jnp.where(holder == devices_at, 1.0, 0.0), axis=1, keepdims=True)
+        start = jnp.sum(jnp.where(holder < devices_at, 1.0, 0.0), axis=1, keepdims=True)
+        table[:, b : b + 1] = length.astype(jnp.int32)
+        table[:, batches + b : batches + b + 1] = start.astype(jnp.int32)
+        table[:, 2 * batches + b : 2 * batches + b + 1] = used.astype(jnp.int32)
         used = used + length
-    flag[0] = (jnp.max(used) > cap).astype(jnp.int32)
+        bent = jnp.zeros((tiles, count), f32)
+        for end in ends:
+            bent = bent + jnp.where(end[b : b + 1, :] == tiles_at, 1.0, 0.0)
+        worst = jnp.maximum(worst, jnp.sum(bent, axis=1, keepdims=True))
+    over = jnp.logical_or(jnp.max(used) > cap, jnp.max(worst) > LANES)
+    flag[0] = over.astype(jnp.int32)
 
     for k in range(chunks):
         for copy in line_out[k]:
@@ -572,6 +576,37 @@
             copy = remote(view, view, plane_send.at[k, j - 1], plane_recv.at[k, j - 1], plane_at((spot + j) % plane_n))
             copy.start()
             plane_out[k].append(copy)
+
+    middle = (width - 1) / 2
+    lowest = (tile * width).astype(f32)
+    highest = lowest + (width - 1)
+    centre, radius = meta[0:batches, :], meta[batches : 2 * batches, :]
+    inverse = 1.0 / radius
+    right_of, left_of = centre <= lowest, centre >= highest
+    near, far = centre - radius, centre + radius
+    smooth = jnp.logical_or(
+        jnp.logical_and(right_of, far >= highest), jnp.logical_and(left_of, near <= lowest)
+    )
+    away = jnp.logical_or(jnp.logical_and(right_of, far <= lowest), jnp.logical_and(left_of, near >= highest))
+    kink = jnp.where(jnp.logical_or(smooth, away), 0.0, 1.0)
+    value = jnp.where(smooth, 1.0 - jnp.abs(lowest + middle - centre) * inverse, 0.0)
+    slope = jnp.where(smooth, jnp.where(right_of, -middle, middle) * inverse, 0.0)
+    padded = jnp.concatenate([kink] + [jnp.zeros_like(kink)] * (16 // batches - 1), axis=0).astype(bf16)
+    counted = jnp.dot(padded, jnp.where(first <= second, 1.0, 0.0).astype(bf16), preferred_element_type=f32)
+    rank = jnp.where(kink > 0.5, counted[:batches] - 1.0, -1.0)
+    for i, rows in enumerate((value * value, 2.0 * value * slope, slope * slope, rank)):
+        taper_in[i * batches : (i + 1) * batches, :] = rows
+    parts = pieces(centre, 2) + pieces(inverse, 3)
+    parts = jnp.concatenate(parts + [jnp.zeros_like(centre)] * (-len(parts) % (16 // batches)), axis=0).astype(bf16)
+    kink_row = lax.broadcasted_iota(jnp.int32, (LANES, count), 0).astype(f32)
+    kink_lane = lax.broadcasted_iota(jnp.int32, (LANES, LANES), 1)
+    columns = jnp.zeros((LANES, LANES), f32)
+    for b in range(batches):
+        ordered = dot_rows(jnp.where(kink_row == rank[b : b + 1, :], 1.0, 0.0).astype(bf16), parts)
+        at = [ordered[:, p * batches + b : p * batches + b + 1] for p in range(5)]
+        columns = jnp.where(kink_lane == b, at[0] + at[1], columns)
+        columns = jnp.where(kink_lane == batches + b, at[2] + at[3] + at[4], columns)
+    kinks[...] = columns
 
     for sends, receives, copy, _ in large:
         pl.when(receives)(copy.wait_recv)
@@ -599,7 +634,7 @@
 
 
 def apply_kernel(
-    cap, width, table, state_in, gathered, meta, out, layers_ref, later_ref, flat, ordered, load_sem,
+    cap, width, table, state_in, gathered, meta, taper_in, kinks, out, layers_ref, later_ref, flat, ordered, load_sem,
 ):
     load = pltpu.make_async_copy(state_in, layers_ref, load_sem)
     load.start()
@@ -618,11 +653,11 @@
 
     def spread(g, carry):
         for b in range(batches):
-            dst, src = table[batches + b, g], g * cap + table[2 * batches + b, g]
+            dst, src = table[g, batches + b], g * cap + table[g, 2 * batches + b]
             for i in range(0, run, 8):
                 ordered[b, pl.ds(dst + i, 8), :] = flat[pl.ds(src + i, 8), :]
 
-            @pl.when(table[b, g] > run)
+            @pl.when(table[g, b] > run)
             def _(b=b, dst=dst, src=src):
                 for i in range(run, cap, 8):
                     ordered[b, pl.ds(dst + i, 8), :] = flat[pl.ds(src + i, 8), :]
@@ -636,6 +671,17 @@
     inverse = 1.0 / meta[batches : 2 * batches, :]
     upright = jnp.concatenate([centre, inverse], axis=0).T
     grid = (first + lax.broadcasted_iota(jnp.int32, (1, width), 1)).astype(jnp.float32)
+
+    middle = (width - 1) / 2
+    offset = lax.broadcasted_iota(jnp.int32, (1, width), 1).astype(jnp.float32)
+    ratio = (offset - middle) * (1.0 / middle)
+    low = lax.broadcasted_iota(jnp.int32, (LANES, LANES), 1) < members
+    kink_row = lax.broadcasted_iota(jnp.int32, (LANES, count), 0).astype(jnp.float32)
+    third = 3 * members
+
+    def bump(positions, here, scale):
+        frac = jnp.maximum(1.0 - jnp.abs(positions - here) * scale, 0.0)
+        return frac * frac
 
     for b in range(batches):
         y = later_ref[b]
@@ -651,30 +697,45 @@
         d_both = jnp.concatenate([d_high, d_low], axis=0)
         y_high = anomaly.astype(jnp.bfloat16).astype(jnp.float32)
         y_low = anomaly - y_high
-        lhs = jnp.concatenate([y_high, y_high, y_low, y_low], axis=0).T.astype(jnp.bfloat16)
+        y_both = jnp.concatenate([y_high, y_low], axis=0).astype(jnp.bfloat16)
         here, scale = upright[:, b : b + 1], upright[:, batches + b : batches + b + 1]
 
-        def taper(positions):
-            frac = jnp.maximum(1.0 - jnp.abs(positions - here) * scale, 0.0)
-            return frac * frac
-
-        def change(x, weight):
+        def stack(x):
             x_high, x_low = halves(x - jnp.sum(x, axis=0, keepdims=True) * (1.0 / members))
-            rhs = jnp.concatenate([x_high, x_low, x_high, x_low], axis=0)
-            gain = jnp.dot(lhs, rhs, preferred_element_type=jnp.float32) * weight
+            return jnp.concatenate([x_high, x_low, x_high, x_low], axis=0)
+
+        if b < batches - 1:
+            lhs = jnp.concatenate([y_high, y_high, y_low, y_low], axis=0).T.astype(jnp.bfloat16)
+        for c in range(b + 1, batches):
+            x = later_ref[c]
+            gain = jnp.dot(lhs, stack(x), preferred_element_type=jnp.float32) * bump(centre[c : c + 1, :], here, scale)
             g_high, g_low = halves(gain)
             one = jnp.dot(d_both, g_high, preferred_element_type=jnp.float32)
             two = jnp.dot(d_high, g_low, preferred_element_type=jnp.float32)
-            return one[:members] + one[members:] + two
-
-        for c in range(b + 1, batches):
-            later_ref[c] += change(later_ref[c], taper(centre[c : c + 1, :]))
-        weight = taper(grid)
+            later_ref[c] = x + (one[:members] + one[members:] + two)
+
+        scaled = [delta * taper_in[i * batches + b : i * batches + b + 1, :] for i in range(3)]
+        scaled = halves(jnp.concatenate(scaled, axis=0))
+        moment = dot_rows(jnp.concatenate(scaled, axis=0), y_both)
+        moment = moment[:third] + moment[third:]
+        moment = halves(moment + pltpu.roll(moment, members, 1))
+        choose = jnp.where(kink_row == taper_in[3 * batches + b : 3 * batches + b + 1, :], 1.0, 0.0).astype(jnp.bfloat16)
+        y_kink = dot_rows(choose, y_both)
+        turned = pltpu.roll(y_kink, members, 1)
+        y_kink = (jnp.where(low, y_kink, turned).astype(jnp.bfloat16), jnp.where(low, turned, y_kink).astype(jnp.bfloat16))
+        left = jnp.concatenate([jnp.concatenate(moment, axis=1), jnp.concatenate(y_kink, axis=1)], axis=0)
+        d_kink = dot_rows(d_both, choose)
+        d_kink = jnp.concatenate([d_kink, jnp.where(kink_row[:, :LANES] < members, d_kink, 0.0)], axis=1).astype(jnp.bfloat16)
+        weight = bump(grid, kinks[:, b : b + 1], kinks[:, batches + b : batches + b + 1])
         if b == 0:
             load.wait()
         for l in range(depth):
             x = layers_ref[l]
-            x = x + change(x, weight)
+            both = jnp.dot(left, stack(x), preferred_element_type=jnp.float32)
+            gain = jnp.concatenate(halves(both[third:] * weight), axis=0)
+            more = jnp.dot(d_kink, gain, preferred_element_type=jnp.float32)
+            x = x + (both[:members] + ratio * (both[members : 2 * members] + ratio * both[2 * members : third]))
+            x = x + (more[:members] + more[members:])
             if b == batches - 1:
                 out[:, l, :] = x
             else:
@@ -753,23 +814,24 @@
     cap = -int(-(mean + 4.0 * mean**0.5) // 16) * 16
     piece = 16 if cap % 32 == 0 else 8
     chunks = cap // (2 * piece)
-    wide = -(-devices // LANES) * LANES
     vmem = pl.BlockSpec(memory_space=pltpu.VMEM)
     smem = pl.BlockSpec(memory_space=pltpu.SMEM)
     hbm = pl.BlockSpec(memory_space=pltpu.HBM)
     f32 = jnp.float32
     dma = pltpu.SemaphoreType.DMA
-    state, gathered, meta, table, flag = pl.pallas_call(
+    state, gathered, meta, taper_in, kinks, table, flag = pl.pallas_call(
         functools.partial(collect_kernel, tiles, layers, cap),
         out_shape=(
             jax.ShapeDtypeStruct((depth, members, width), f32),
             jax.ShapeDtypeStruct((chunks, devices, piece, LANES), f32),
             jax.ShapeDtypeStruct((4 * batches, count), f32),
-            jax.ShapeDtypeStruct((3 * batches, wide), jnp.int32),
+            jax.ShapeDtypeStruct((4 * batches, count), f32),
+            jax.ShapeDtypeStruct((LANES, LANES), f32),
+            jax.ShapeDtypeStruct((devices, 3 * batches), jnp.int32),
             jax.ShapeDtypeStruct((1,), jnp.int32),
         ),
         in_specs=[hbm] * 9,
-        out_specs=(hbm, vmem, vmem, vmem, smem),
+        out_specs=(hbm, vmem, vmem, vmem, vmem, vmem, smem),
         scratch_shapes=[
             pltpu.VMEM((depth, members, width), f32),
             dma,
@@ -796,7 +858,7 @@
         return pl.pallas_call(
             functools.partial(apply_kernel, cap, width),
             out_shape=jax.ShapeDtypeStruct((members, depth, width), f32),
-            in_specs=[smem, hbm, vmem, vmem],
+            in_specs=[smem, hbm, vmem, vmem, vmem, vmem],
             out_specs=vmem,
             scratch_shapes=[
                 pltpu.VMEM((depth, members, width), f32),
@@ -807,7 +869,7 @@
             ],
             compiler_params=pltpu.CompilerParams(vmem_limit_bytes=48 * 2**20),
             name="apply",
-        )(table, state, gathered, meta)
+        )(table, state, gathered, meta, taper_in, kinks)
 
     def slow():
         return slow_shards(ensemble, diff_x, diff_z, cour_x, cour_z, obs_cell, obs_radius, obs_value, obs_var)

time: 35.4 us -> 34.3 us (0.969)
  Pallas kernels: 34 us -> 32.5 us
  local copies, waits for them, and re-layouts: 0.07 us -> 0.65 us
    pallas_call x1, Pallas kernels: 14.4 us -> 12.9 us  [fast(): pl.pallas_call(functools.partial(apply_kernel, cap, width), out_shape=jax...]
    unnamed x18, local copies, waits for them, and re-layouts: 0.07 us -> 0.65 us
where the time goes in v2:
time: 34.3 us; the launch traced here: 34 us
  Pallas kernels  32.5 us (95%)
  between operations  0.85 us (2%)
  local copies, waits for them, and re-layouts  0.65 us (2%)
    pallas_call x1, Pallas kernels, shards(): pl.pallas_call(functools.partial(collect_kernel, tiles, layers, cap), out...  19.6 us
    pallas_call x1, Pallas kernels, fast(): pl.pallas_call(functools.partial(apply_kernel, cap, width), out_shape=jax...  12.9 us

profile of v2, /device:TPU:1, one launch (start us, length us, event | category | flops | bytes accessed | tf_op | source)
XLA Modules:
  0.0 34.0 jit_solution(17718169987914540501)
XLA Ops:
  0.0 0.0 copy-start
  0.0 0.0 copy-start.3
  0.0 0.0 copy-start.4
  0.0 0.0 copy-start.5
  0.0 0.0 copy-start.6
  0.0 0.0 copy-start.7
  0.0 0.0 copy-start.8
  0.0 19.6 %collect.1 = (f32[4,64,512]{2,1,0:T(8,128)S(1)}, f32[3,32,16,128]{3,2,1,0:T(8,128)S(1)}, f32[16,512]{1,0:T(8,128)S(1)}, f32[16,512]{1,0:T(8,128)S(1)}, f32[128,1...) custom-call(f32[64,4,512]{2,1,0:T(4,128)} %ens_in.1, f32[4,512]{1,0:T(4,128)} %dx_in.1, f32[4,512]{1,0:T(4,128)} %dz_in.1, ...), custom_call_target="tpu_custom_call" | custom-call | tf_op jit(solution)/shard_map/collect/pallas_call | solution.py:822
  19.6 0.0 copy-start.2
  20.2 0.0 copy-start.1
  20.2 0.0 copy-done
  20.3 0.0 copy-done.3
  20.3 0.0 copy-done.4
  20.3 0.0 copy-done.5
  20.3 0.0 copy-done.6
  20.3 0.0 copy-done.7
  20.3 0.0 copy-done.8
  20.3 0.0 copy-done.2
  20.3 0.6 %copy-done.1 = s32[4,512]{1,0:T(4,128)S(1)} copy-done((s32[4,512]{1,0:T(4,128)S(1)}, s32[4,512]{1,0:T(4,128)}, u32[]{:S(2)}) %copy-start.1) | copy-done | bytes 8216
  20.9 12.9 %conditional.1 = (f32[64,4,512]{2,1,0:T(4,128)}) conditional(s32[]{:T(128)} %bitcast, (s32[32,12]{1,0:T(8,128)S(1)}, f32[4,64,512]{2,1,0:T(8,128)S(1)}, f32[3,32,16,128]{3,2,1,0:T(8,128)S(1)}, f32[16,512]{1,0:T(8,128)S(1)}, f32[16,512]{1,0:T(8,128)S(1)}, /*index=5*/f32[128,128]{1,0:T(8,128)S(1)}) %tuple.11, (f32[64,4,512]{2,1,0:T(4,128)S(1)}, ...), branch_computations={%region_0.0_spmd, %region_1.0_spmd} | conditional | bytes 8 | solution.py:877
  20.9 12.9 %apply.1 = f32[64,4,512]{2,1,0:T(4,128)} custom-call(s32[32,12]{1,0:T(8,128)S(1)} %get-tuple-element.38.table, f32[4,64,512]{2,1,0:T(8,128)S(1)} %get-tuple-element.39.state_in, f32[3,32,16,128]{3,2,1,0:T(8,128)S(1)} %get-tuple-element.40.gathered, f32[16,512]{1,0:T(8,128)S(1)} %get-tuple-element.41.meta, f32[16,512]{1,0:T(8,128)S(1)} %get-tuple-element.42.taper_in, ...), custom_call_target="tpu_custom_call" | custom-call | tf_op jit(solution)/shard_map/cond/branch_0_fun/apply/pallas_call | solution.py:858
Async XLA Ops:
  0.0 20.2 %copy-start = (f32[64,4,512]{2,1,0:T(4,128)S(1)}, f32[64,4,512]{2,1,0:T(4,128)}, u32[]{:S(2)}) copy-start(f32[64,4,512]{2,1,0:T(4,128)} %ens_in.1) | copy-start | bytes 1572868
  0.0 20.3 %copy-start.3 = (f32[4,512]{1,0:T(4,128)S(1)}, f32[4,512]{1,0:T(4,128)}, u32[]{:S(2)}) copy-start(f32[4,512]{1,0:T(4,128)} %dz_in.1) | copy-start | bytes 24580
  0.0 20.3 %copy-start.4 = (f32[4,512]{1,0:T(4,128)S(1)}, f32[4,512]{1,0:T(4,128)}, u32[]{:S(2)}) copy-start(f32[4,512]{1,0:T(4,128)} %cx_in.1) | copy-start | bytes 24580
  0.0 20.3 %copy-start.5 = (f32[4,512]{1,0:T(4,128)S(1)}, f32[4,512]{1,0:T(4,128)}, u32[]{:S(2)}) copy-start(f32[4,512]{1,0:T(4,128)} %cz_in.1) | copy-start | bytes 24580
  0.0 20.3 %copy-start.6 = (s32[4,512]{1,0:T(4,128)S(1)}, s32[4,512]{1,0:T(4,128)}, u32[]{:S(2)}) copy-start(s32[4,512]{1,0:T(4,128)} %radius_in.1) | copy-start | bytes 24580
  0.0 20.3 %copy-start.7 = (f32[4,512]{1,0:T(4,128)S(1)}, f32[4,512]{1,0:T(4,128)}, u32[]{:S(2)}) copy-start(f32[4,512]{1,0:T(4,128)} %value_in.1) | copy-start | bytes 24580
  0.0 20.3 %copy-start.8 = (f32[4,512]{1,0:T(4,128)S(1)}, f32[4,512]{1,0:T(4,128)}, u32[]{:S(2)}) copy-start(f32[4,512]{1,0:T(4,128)} %var_in.1) | copy-start | bytes 24580
  19.6 0.7 %copy-start.2 = (f32[4,512]{1,0:T(4,128)S(1)}, f32[4,512]{1,0:T(4,128)}, u32[]{:S(2)}) copy-start(f32[4,512]{1,0:T(4,128)} %dx_in.1) | copy-start | bytes 24580
  20.2 0.7 %copy-start.1 = (s32[4,512]{1,0:T(4,128)S(1)}, s32[4,512]{1,0:T(4,128)}, u32[]{:S(2)}) copy-start(s32[4,512]{1,0:T(4,128)} %cell_in.1) | copy-start | bytes 24580

commit v3 on v1

--- a/solution.py
+++ b/solution.py
@@ -328,11 +328,11 @@
 
 
 def collect_kernel(
-    tiles, layers, cap, ens_in, dx_in, dz_in, cx_in, cz_in, cell_in, radius_in, value_in, var_in,
-    state_out, gathered, meta, table, flag,
+    tiles, layers, cap, cuts, bends, ens_in, dx_in, dz_in, cx_in, cz_in, cell_in, radius_in, value_in, var_in,
+    state_out, flat, meta, taper_in, kinks, tapers, table, flag,
     state, state_sem, ens, diff_x, diff_z, cour_x, cour_z, obs_cell, obs_radius, obs_value, obs_var, load_sem,
     cells, edge_w, edge_e, halo_w, halo_e, near_u, near_d, part_u, part_d, halo_u, halo_d,
-    hop_send, hop_recv, line_send, line_recv, plane_send, plane_recv, core_send, core_recv,
+    gathered, hop_send, hop_recv, line_send, line_recv, plane_send, plane_recv, core_send, core_recv,
 ):
     loads = []
     for i, (src, dst) in enumerate(
@@ -517,10 +517,7 @@
     core_of, row_of, line_of = cell_tile & 1, divide(cell_tile, 2) & 1, divide(cell_tile, 4)
     owner = (core_of * plane_n + cell_layer * 2 + row_of) * line_n + line_of
     key = (owner * count + lax.broadcasted_iota(jnp.int32, (batches, count), 1)).astype(f32)
-    both = jnp.concatenate([key, owner.astype(f32)], axis=0)
-    if 2 * batches % 8:
-        both = jnp.concatenate([both, jnp.zeros((8 - 2 * batches % 8, count), f32)], axis=0)
-    upright = both.T
+    upright = jnp.concatenate([key, jnp.zeros_like(key)], axis=0).T
 
     def pieces(values, n):
         out = []
@@ -536,9 +533,12 @@
     parts = []
     for values, n in fields:
         parts.extend(pieces(values, n))
-    wide = table.shape[1]
-    lane_d = lax.broadcasted_iota(jnp.int32, (count, wide), 1).astype(f32)
-    used = jnp.zeros((1, wide), f32)
+    devices_at = lax.broadcasted_iota(jnp.int32, (devices, count), 0)
+    cuts_at = lax.broadcasted_iota(jnp.int32, (tiles * cuts, count), 0)
+    ends = [divide(cell_col + obs_radius[...] * step, width // cuts) for step in (-1, 0, 1)]
+    used = jnp.zeros((devices, 1), f32)
+    worst = jnp.zeros((tiles * cuts, 1), f32)
+    longest = jnp.zeros((devices, 1), f32)
     if len(parts) * batches % 16:
         parts.append(jnp.zeros((16 - len(parts) * batches % 16, count), f32))
     parts = jnp.concatenate(parts, axis=0).astype(bf16)
@@ -555,14 +555,22 @@
                 total = total + ordered[(i + p) * batches + b : (i + p) * batches + b + 1, :]
             meta[f * batches + b : f * batches + b + 1, :] = total
             i += n
-        holder = upright[:, batches + b : batches + b + 1]
-        length = jnp.sum(jnp.where(holder == lane_d, 1.0, 0.0), axis=0, keepdims=True)
-        start = jnp.sum(jnp.where(holder < lane_d, 1.0, 0.0), axis=0, keepdims=True)
-        table[b : b + 1, :] = length.astype(jnp.int32)
-        table[batches + b : batches + b + 1, :] = start.astype(jnp.int32)
-        table[2 * batches + b : 2 * batches + b + 1, :] = used.astype(jnp.int32)
+        holder = owner[b : b + 1, :]
+        length = jnp.sum(jnp.where(holder == devices_at, 1.0, 0.0), axis=1, keepdims=True)
+        start = jnp.sum(jnp.where(holder < devices_at, 1.0, 0.0), axis=1, keepdims=True)
+        table[:, b : b + 1] = length.astype(jnp.int32)
+        table[:, batches + b : batches + b + 1] = start.astype(jnp.int32)
+        table[:, 2 * batches + b : 2 * batches + b + 1] = used.astype(jnp.int32)
         used = used + length
-    flag[0] = (jnp.max(used) > cap).astype(jnp.int32)
+        longest = jnp.maximum(longest, length)
+        bent = jnp.zeros((tiles * cuts, count), f32)
+        for end in ends:
+            bent = bent + jnp.where(end[b : b + 1, :] == cuts_at, 1.0, 0.0)
+        worst = jnp.maximum(worst, jnp.sum(bent, axis=1, keepdims=True))
+    longest = jnp.max(longest, axis=0, keepdims=True)
+    table[:, 3 * batches : 3 * batches + 1] = jnp.broadcast_to(longest, (devices, 1)).astype(jnp.int32)
+    over = jnp.logical_or(jnp.max(used) > cap, jnp.max(worst) > bends)
+    flag[0] = over.astype(jnp.int32)
 
     for k in range(chunks):
         for copy in line_out[k]:
@@ -573,12 +581,70 @@
             copy.start()
             plane_out[k].append(copy)
 
+    part_w = width // cuts
+    middle = (part_w - 1) / 2
+    centre, radius = meta[0:batches, :], meta[batches : 2 * batches, :]
+    inverse = 1.0 / radius
+    near, far = centre - radius, centre + radius
+    bent = []
+    for c in range(cuts):
+        lowest = (tile * width + c * part_w).astype(f32)
+        highest = lowest + (part_w - 1)
+        right_of, left_of = centre <= lowest, centre >= highest
+        smooth = jnp.logical_or(
+            jnp.logical_and(right_of, far >= highest), jnp.logical_and(left_of, near <= lowest)
+        )
+        away = jnp.logical_or(jnp.logical_and(right_of, far <= lowest), jnp.logical_and(left_of, near >= highest))
+        bent.append(jnp.where(jnp.logical_or(smooth, away), 0.0, 1.0))
+        value = jnp.where(smooth, 1.0 - jnp.abs(lowest + middle - centre) * inverse, 0.0)
+        slope = jnp.where(smooth, jnp.where(right_of, -middle, middle) * inverse, 0.0)
+        for i, rows in enumerate((value * value, 2.0 * value * slope, slope * slope)):
+            start = (c * 4 + i) * batches
+            taper_in[start : start + batches, :] = rows
+    padded = jnp.concatenate(bent + [jnp.zeros_like(centre)] * (-cuts % (16 // batches)), axis=0).astype(bf16)
+    counted = jnp.dot(padded, jnp.where(first <= second, 1.0, 0.0).astype(bf16), preferred_element_type=f32)
+    ranks = []
+    for c in range(cuts):
+        ranks.append(jnp.where(bent[c] > 0.5, counted[c * batches : (c + 1) * batches] - 1.0, -1.0))
+        taper_in[(c * 4 + 3) * batches : (c * 4 + 4) * batches, :] = ranks[c]
+    parts = pieces(centre, 2) + pieces(inverse, 3)
+    parts = jnp.concatenate(parts + [jnp.zeros_like(centre)] * (-len(parts) % (16 // batches)), axis=0).astype(bf16)
+    kink_row = lax.broadcasted_iota(jnp.int32, (bends, count), 0).astype(f32)
+    grid = (tile * width + lax.broadcasted_iota(jnp.int32, (1, width), 1)).astype(f32)
+
+    def bump(positions, here, scale):
+        frac = jnp.maximum(1.0 - jnp.abs(positions - here) * scale, 0.0)
+        return frac * frac
+
+    for b in range(batches):
+        choose = [jnp.where(kink_row == ranks[c][b : b + 1, :], 1.0, 0.0).astype(bf16) for c in range(cuts)]
+        ordered = dot_rows(jnp.concatenate(choose, axis=0), parts)
+        at = [ordered[:, p * batches + b : p * batches + b + 1] for p in range(5)]
+        kink_c, kink_i = at[0] + at[1], at[2] + at[3] + at[4]
+        for c in range(cuts):
+            rows = slice(c * bends, (c + 1) * bends)
+            kinks[b, c] = bump(grid[:, c * part_w : (c + 1) * part_w], kink_c[rows], kink_i[rows])
+    upright = jnp.concatenate([centre, inverse], axis=0).T
+    i = 0
+    for b in range(batches):
+        for c in range(b + 1, batches):
+            tapers[i] = bump(centre[c : c + 1, :], upright[:, b : b + 1], upright[:, batches + b : batches + b + 1])
+            i += 1
+
     for sends, receives, copy, _ in large:
         pl.when(receives)(copy.wait_recv)
     state[0] += halo_u[...] * coef_u
     state[depth - 1] += halo_d[...] * coef_d
     keep = pltpu.make_async_copy(state, state_out, state_sem)
     keep.start()
+
+    def unpack(k, side):
+        for i in range(devices // 2):
+            g = side * (devices // 2) + i
+            rows = gathered[k, g]
+            at = pl.multiple_of(g * cap + 2 * piece * k, 8)
+            flat[pl.ds(at, piece), :] = rows
+            flat[pl.ds(at + piece, piece), :] = pltpu.roll(rows, members, 1)
 
     for k in range(chunks):
         for copy in plane_out[k]:
@@ -587,8 +653,10 @@
         copy = remote(view, view, core_send.at[k], core_recv.at[k], pair)
         copy.start()
         core_out[k].append(copy)
+        unpack(k, core)
     for k in range(chunks):
         core_out[k][0].wait_recv()
+        unpack(k, 1 - core)
     for group in (line_out, plane_out, core_out):
         for copies in group:
             for copy in copies:
@@ -599,43 +667,45 @@
 
 
 def apply_kernel(
-    cap, width, table, state_in, gathered, meta, out, layers_ref, later_ref, flat, ordered, load_sem,
+    cap, table, state_in, flat, meta, taper_in, kinks, tapers, out, layers_ref, later_ref, ordered, load_sem,
 ):
     load = pltpu.make_async_copy(state_in, layers_ref, load_sem)
     load.start()
     depth, members, _ = layers_ref.shape
     batches, _, count = later_ref.shape
-    chunks, devices, piece, _ = gathered.shape
-    first = lax.axis_index("tile") * width
-    for k in range(chunks):
-        for g in range(devices):
-            rows = gathered[k, g]
-            at = g * cap + 2 * piece * k
-            flat[at : at + piece, :] = rows
-            flat[at + piece : at + 2 * piece, :] = pltpu.roll(rows, members, 1)
-
-    run = min(cap, (count // devices + 7) // 8 * 8 + 8)
-
-    def spread(g, carry):
-        for b in range(batches):
-            dst, src = table[batches + b, g], g * cap + table[2 * batches + b, g]
-            for i in range(0, run, 8):
-                ordered[b, pl.ds(dst + i, 8), :] = flat[pl.ds(src + i, 8), :]
-
-            @pl.when(table[b, g] > run)
-            def _(b=b, dst=dst, src=src):
-                for i in range(run, cap, 8):
+    devices = table.shape[0]
+    mean = count / devices
+    run = min(cap, -int(-(mean + 4.0 * mean**0.5) // 8) * 8)
+
+    def spread(size):
+        def step(g, carry):
+            for b in range(batches):
+                dst, src = table[g, batches + b], g * cap + table[g, 2 * batches + b]
+                for i in range(0, size, 8):
                     ordered[b, pl.ds(dst + i, 8), :] = flat[pl.ds(src + i, 8), :]
-
-        return carry
-
-    lax.fori_loop(0, devices, spread, 0)
+            return carry
+
+        return step
+
+    lax.fori_loop(0, devices, spread(run), 0, unroll=4)
+
+    @pl.when(table[0, 3 * batches] > run)
+    def _():
+        lax.fori_loop(0, devices, spread(cap), 0)
+
     for b in range(batches):
         later_ref[b] = ordered[b, :count, :].T[:members]
-    centre = meta[0:batches, :]
-    inverse = 1.0 / meta[batches : 2 * batches, :]
-    upright = jnp.concatenate([centre, inverse], axis=0).T
-    grid = (first + lax.broadcasted_iota(jnp.int32, (1, width), 1)).astype(jnp.float32)
+    _, cuts, bends, part_w = kinks.shape
+    middle = (part_w - 1) / 2
+    offset = lax.broadcasted_iota(jnp.int32, (1, part_w), 1).astype(jnp.float32)
+    ratio = (offset - middle) * (1.0 / middle)
+    ratio = jnp.concatenate([ratio] * depth, axis=1)
+    third = 3 * members
+    both_low = lax.broadcasted_iota(jnp.int32, (third, LANES), 1) < members
+    low = lax.broadcasted_iota(jnp.int32, (2 * members, LANES), 1) < members
+    top = lax.broadcasted_iota(jnp.int32, (2 * members, LANES), 0) < members
+    kink_row = lax.broadcasted_iota(jnp.int32, (bends, count), 0).astype(jnp.float32)
+    pair = 0
 
     for b in range(batches):
         y = later_ref[b]
@@ -651,34 +721,77 @@
         d_both = jnp.concatenate([d_high, d_low], axis=0)
         y_high = anomaly.astype(jnp.bfloat16).astype(jnp.float32)
         y_low = anomaly - y_high
-        lhs = jnp.concatenate([y_high, y_high, y_low, y_low], axis=0).T.astype(jnp.bfloat16)
-        here, scale = upright[:, b : b + 1], upright[:, batches + b : batches + b + 1]
-
-        def taper(positions):
-            frac = jnp.maximum(1.0 - jnp.abs(positions - here) * scale, 0.0)
-            return frac * frac
-
-        def change(x, weight):
+        y_both = jnp.concatenate([y_high, y_low], axis=0).astype(jnp.bfloat16)
+
+        def stack(x):
             x_high, x_low = halves(x - jnp.sum(x, axis=0, keepdims=True) * (1.0 / members))
-            rhs = jnp.concatenate([x_high, x_low, x_high, x_low], axis=0)
-            gain = jnp.dot(lhs, rhs, preferred_element_type=jnp.float32) * weight
-            g_high, g_low = halves(gain)
-            one = jnp.dot(d_both, g_high, preferred_element_type=jnp.float32)
-            two = jnp.dot(d_high, g_low, preferred_element_type=jnp.float32)
-            return one[:members] + one[members:] + two
-
-        for c in range(b + 1, batches):
-            later_ref[c] += change(later_ref[c], taper(centre[c : c + 1, :]))
-        weight = taper(grid)
+            return jnp.concatenate([x_high, x_high, x_low, x_low], axis=0)
+
+        def twice(x):
+            return jnp.concatenate([x, x], axis=1).astype(jnp.bfloat16)
+
+        if b < batches - 1:
+            lhs = twice(jnp.concatenate([y_high, y_low], axis=0).T)
+        rest = range(b + 1, batches)
+        crosses = [jnp.dot(lhs, stack(later_ref[c]), preferred_element_type=jnp.float32) for c in rest]
+        gains = [halves(cross * tapers[pair + i]) for i, cross in enumerate(crosses)]
+        pair += len(rest)
+        ones = [jnp.dot(d_both, high, preferred_element_type=jnp.float32) for high, _ in gains]
+        twos = [jnp.dot(d_high, lower, preferred_element_type=jnp.float32) for _, lower in gains]
+        for i, c in enumerate(rest):
+            later_ref[c] += ones[i][:members] + ones[i][members:] + twos[i]
+
+        scaled = []
+        for c in range(cuts):
+            for i in range(3):
+                row = (c * 4 + i) * batches + b
+                scaled.append(delta * taper_in[row : row + 1, :])
+        moments = dot_rows(jnp.concatenate(halves(jnp.concatenate(scaled, axis=0)), axis=0), y_both)
+        choose = []
+        for c in range(cuts):
+            row = (c * 4 + 3) * batches + b
+            choose.append(jnp.where(kink_row == taper_in[row : row + 1, :], 1.0, 0.0).astype(jnp.bfloat16))
+        choose = jnp.concatenate(choose, axis=0)
+        y_kink = dot_rows(choose, y_both)
+        d_kink = dot_rows(d_both, choose)
+        turned = pltpu.roll(d_kink, members, 1)
+        lefts, rights = [], []
         if b == 0:
             load.wait()
-        for l in range(depth):
-            x = layers_ref[l]
-            x = x + change(x, weight)
-            if b == batches - 1:
-                out[:, l, :] = x
+        for c in range(cuts):
+            moment = moments[c * third : (c + 1) * third] + moments[(cuts + c) * third : (cuts + c + 1) * third]
+            m_high, m_low = halves(moment + pltpu.roll(moment, members, 1))
+            moment = jnp.where(both_low, m_high.astype(jnp.float32), m_low.astype(jnp.float32))
+            left = twice(jnp.concatenate([moment, y_kink[c * bends : (c + 1) * bends]], axis=0))
+            if cuts == 1:
+                right = jnp.concatenate([d_kink, jnp.where(top, d_kink, 0.0)], axis=1)
+            elif c == 0:
+                right = jnp.where(low, d_kink, jnp.where(top, turned, 0.0))
             else:
-                layers_ref[l] = x
+                right = jnp.where(low, turned, jnp.where(top, d_kink, 0.0))
+            right = right.astype(jnp.bfloat16)
+            lefts.append(left)
+            rights.append(right)
+        olds, firsts, gains, seconds = [], [], [], []
+        for c in range(cuts):
+            columns = slice(c * part_w, (c + 1) * part_w)
+            olds.append(jnp.concatenate([layers_ref[l, :, columns] for l in range(depth)], axis=1))
+            firsts.append(jnp.dot(lefts[c], stack(olds[c]), preferred_element_type=jnp.float32))
+        for c in range(cuts):
+            weight = jnp.concatenate([kinks[b, c]] * depth, axis=1)
+            gains.append(jnp.concatenate(halves(firsts[c][third:] * weight), axis=0))
+        for c in range(cuts):
+            seconds.append(jnp.dot(rights[c], gains[c], preferred_element_type=jnp.float32))
+        for c in range(cuts):
+            both, more = firsts[c], seconds[c]
+            x = olds[c] + (both[:members] + ratio * (both[members : 2 * members] + ratio * both[2 * members : third]))
+            x = x + (more[:members] + more[members:])
+            columns = slice(c * part_w, (c + 1) * part_w)
+            for l in range(depth):
+                if b == batches - 1:
+                    out[:, l, columns] = x[:, l * part_w : (l + 1) * part_w]
+                else:
+                    layers_ref[l, :, columns] = x[:, l * part_w : (l + 1) * part_w]
 
 
 def slow_shards(ensemble, diff_x, diff_z, cour_x, cour_z, obs_cell, obs_radius, obs_value, obs_var):
@@ -753,23 +866,26 @@
     cap = -int(-(mean + 4.0 * mean**0.5) // 16) * 16
     piece = 16 if cap % 32 == 0 else 8
     chunks = cap // (2 * piece)
-    wide = -(-devices // LANES) * LANES
+    cuts, bends = (2, 64) if width % (2 * LANES) == 0 else (1, LANES)
     vmem = pl.BlockSpec(memory_space=pltpu.VMEM)
     smem = pl.BlockSpec(memory_space=pltpu.SMEM)
     hbm = pl.BlockSpec(memory_space=pltpu.HBM)
     f32 = jnp.float32
     dma = pltpu.SemaphoreType.DMA
-    state, gathered, meta, table, flag = pl.pallas_call(
-        functools.partial(collect_kernel, tiles, layers, cap),
+    state, flat, meta, taper_in, kinks, tapers, table, flag = pl.pallas_call(
+        functools.partial(collect_kernel, tiles, layers, cap, cuts, bends),
         out_shape=(
             jax.ShapeDtypeStruct((depth, members, width), f32),
-            jax.ShapeDtypeStruct((chunks, devices, piece, LANES), f32),
+            jax.ShapeDtypeStruct((devices * cap + cap, LANES), f32),
             jax.ShapeDtypeStruct((4 * batches, count), f32),
-            jax.ShapeDtypeStruct((3 * batches, wide), jnp.int32),
+            jax.ShapeDtypeStruct((cuts * 4 * batches, count), f32),
+            jax.ShapeDtypeStruct((batches, cuts, bends, width // cuts), f32),
+            jax.ShapeDtypeStruct((batches * (batches - 1) // 2, count, count), f32),
+            jax.ShapeDtypeStruct((devices, 3 * batches + 1), jnp.int32),
             jax.ShapeDtypeStruct((1,), jnp.int32),
         ),
         in_specs=[hbm] * 9,
-        out_specs=(hbm, vmem, vmem, vmem, smem),
+        out_specs=(hbm, vmem, vmem, vmem, vmem, vmem, vmem, smem),
         scratch_shapes=[
             pltpu.VMEM((depth, members, width), f32),
             dma,
@@ -782,6 +898,7 @@
             *[pltpu.VMEM((8, LANES), f32)] * 4,
             *[pltpu.VMEM((cap // 2, LANES), f32)] * 4,
             *[pltpu.VMEM((members, width), f32)] * 2,
+            pltpu.VMEM((chunks, devices, piece, LANES), f32),
             dma((6,)),
             dma((6,)),
             *[dma((chunks, max(line_n - 1, 1)))] * 2,
@@ -794,20 +911,19 @@
 
     def fast():
         return pl.pallas_call(
-            functools.partial(apply_kernel, cap, width),
+            functools.partial(apply_kernel, cap),
             out_shape=jax.ShapeDtypeStruct((members, depth, width), f32),
-            in_specs=[smem, hbm, vmem, vmem],
+            in_specs=[smem, hbm, vmem, vmem, vmem, vmem, vmem],
             out_specs=vmem,
             scratch_shapes=[
                 pltpu.VMEM((depth, members, width), f32),
                 pltpu.VMEM((batches, members, count), f32),
-                pltpu.VMEM((devices * cap + cap, LANES), f32),
                 pltpu.VMEM((batches, count + cap, LANES), f32),
                 dma,
             ],
             compiler_params=pltpu.CompilerParams(vmem_limit_bytes=48 * 2**20),
             name="apply",
-        )(table, state, gathered, meta)
+        )(table, state, flat, meta, taper_in, kinks, tapers)
 
     def slow():
         return slow_shards(ensemble, diff_x, diff_z, cour_x, cour_z, obs_cell, obs_radius, obs_value, obs_var)

time: 35.4 us -> 29.2 us (0.82)
  Pallas kernels: 34 us -> 27.9 us
    pallas_call x2, Pallas kernels: 34 us -> 27.9 us  [the longest x1 19.6 us: shards(): pl.pallas_call(functools.partial(collect_kernel, tiles, layers, cap, cuts...]
where the time goes in v3:
time: 29.2 us; the launch traced here: 29 us
  Pallas kernels  27.9 us (96%)
  between operations  0.81 us (3%)
    pallas_call x1, Pallas kernels, shards(): pl.pallas_call(functools.partial(collect_kernel, tiles, layers, cap, cuts...  19.6 us
    pallas_call x1, Pallas kernels, fast(): pl.pallas_call(functools.partial(apply_kernel, cap), out_shape=jax.ShapeD...  8.31 us

profile of v3, /device:TPU:1, one launch (start us, length us, event | category | flops | bytes accessed | tf_op | source)
XLA Modules:
  0.0 29.0 jit_solution(9808584313812499301)
XLA Ops:
  0.0 19.6 %collect.1 = (f32[4,64,512]{2,1,0:T(8,128)S(1)}, f32[3168,128]{1,0:T(8,128)S(1)}, f32[16,512]{1,0:T(8,128)S(1)}, f32[32,512]{1,0:T(8,128)S(1)}, f32[4,2,64,256]{...) custom-call(f32[64,4,512]{2,1,0:T(4,128)} %ens_in.1, f32[4,512]{1,0:T(4,128)} %dx_in.1, ...), custom_call_target="tpu_custom_call" | custom-call | tf_op jit(solution)/shard_map/collect/pallas_call | solution.py:875
  20.3 8.5 %conditional.1 = (f32[64,4,512]{2,1,0:T(4,128)}) conditional(s32[]{:T(128)} %bitcast, (s32[32,13]{1,0:T(8,128)S(1)}, f32[4,64,512]{2,1,0:T(8,128)S(1)}, f32[3168,128]{1,0:T(8,128)S(1)}, f32[16,512]{1,0:T(8,128)S(1)}, f32[32,512]{1,0:T(8,128)S(1)}, /*index=5*/f32[4,2,64,256]{3,2,1,0:T(8,128)S(1)}, f32[6,512,512]{2,1,0:T(8,128)S(1)}) %tuple.11, ...), branch_computations={%region_0.0_spmd, %region_1.0_spmd} | conditional | bytes 8 | solution.py:931
  20.3 8.3 %apply.1 = f32[64,4,512]{2,1,0:T(4,128)} custom-call(s32[32,13]{1,0:T(8,128)S(1)} %get-tuple-element.40.table, f32[4,64,512]{2,1,0:T(8,128)S(1)} %get-tuple-element.41.state_in, f32[3168,128]{1,0:T(8,128)S(1)} %get-tuple-element.42.flat, f32[16,512]{1,0:T(8,128)S(1)} %get-tuple-element.43.meta, f32[32,512]{1,0:T(8,128)S(1)} %get-tuple-element.44.taper_in, ...), custom_call_target="tpu_custom_call" | custom-call | tf_op jit(solution)/shard_map/cond/branch_0_fun/apply/pallas_call | solution.py:913

commit v4 on v3

--- a/solution.py
+++ b/solution.py
@@ -374,38 +374,58 @@
     cell_tile, cell_layer = divide(cell_col, width), divide(cell_row, depth)
     local_col, local_row = cell_col - cell_tile * width, cell_row - cell_layer * depth
     here = cell_tile == tile
+    up_rim = jnp.logical_and(local_row == 0, cell_layer > 0)
+    down_rim = jnp.logical_and(local_row == depth - 1, cell_layer < layers - 1)
+    side_rim = jnp.logical_or(local_col == 0, local_col == width - 1)
+    rim = jnp.where(jnp.logical_or(side_rim, jnp.logical_or(up_rim, down_rim)), 1.0, 0.0)
     groups = [
-        jnp.where(jnp.logical_and(here, cell_layer == layer + step), 1.0, 0.0) for step in (0, -1, 1)
+        jnp.where(jnp.logical_and(here, cell_layer == layer + step), share, 0.0)
+        for step, share in ((0, 1.0 - rim), (0, rim), (-1, rim), (1, rim))
     ]
-    masks = jnp.concatenate(groups + [jnp.zeros_like(groups[0])], axis=0).astype(bf16)
+    masks = jnp.concatenate(groups, axis=0).astype(bf16)
     first = lax.broadcasted_iota(jnp.int32, (count, count), 0)
     second = lax.broadcasted_iota(jnp.int32, (count, count), 1)
     running = jnp.dot(masks, jnp.where(first <= second, 1.0, 0.0).astype(bf16), preferred_element_type=f32)
     code = (local_row * width + local_col + 1).astype(f32)
-    slot = lax.broadcasted_iota(jnp.int32, (cap, count), 0).astype(f32)
-    lane_w = lax.broadcasted_iota(jnp.int32, (cap, width), 1)
-    found = []
-    for k, edge in enumerate((None, depth - 1, 0)):
-        before_ = jnp.zeros((1, 1), f32)
-        total = jnp.zeros((cap, count), f32)
+    late = 2 * piece
+    ranks, sums = [], []
+    for k in range(4):
+        total = jnp.zeros((1, 1), f32)
+        rows = []
         for b in range(batches):
             i = k * batches + b
-            wanted = groups[k][b : b + 1, :] > 0.5
-            if edge is not None:
-                wanted = jnp.logical_and(wanted, local_row[b : b + 1, :] == edge)
-            rank = jnp.where(wanted, running[i : i + 1, :] + (before_ - 1.0), -1.0)
-            total = total + jnp.where(rank == slot, code[b : b + 1, :], 0.0)
-            before_ = before_ + running[i : i + 1, count - 1 : count]
+            rows.append(running[i : i + 1, :] + (total - 1.0))
+            total = total + running[i : i + 1, count - 1 : count]
+        ranks.append(rows)
+        sums.append(total)
+
+    def locate(size, slots_of):
+        slot = lax.broadcasted_iota(jnp.int32, (size, count), 0).astype(f32)
+        lanes = lax.broadcasted_iota(jnp.int32, (size, width), 1)
+        total = jnp.zeros((size, count), f32)
+        for b in range(batches):
+            total = total + jnp.where(slots_of(b) == slot, code[b : b + 1, :], 0.0)
         cell = jnp.sum(total, axis=1, keepdims=True).astype(jnp.int32) - 1
         at_row = divide(cell, width)
         at_col = jnp.where(cell >= 0, cell - at_row * width, -1)
-        found.append((at_row, at_col, jnp.where(lane_w == at_col, 1.0, 0.0)))
+        return at_row, at_col, jnp.where(lanes == at_col, 1.0, 0.0)
+
+    def facing(k, edge):
+        def slots_of(b):
+            wanted = jnp.logical_and(groups[k][b : b + 1, :] > 0.5, local_row[b : b + 1, :] == edge)
+            return jnp.where(wanted, ranks[k][b] + (late - sums[k]), -1.0)
+
+        return locate(late, slots_of)[2]
+
+    def own(b):
+        rim_slot = jnp.where(groups[1][b : b + 1, :] > 0.5, ranks[1][b] + (cap - sums[1]), -1.0)
+        return jnp.where(groups[0][b : b + 1, :] > 0.5, ranks[0][b], rim_slot)
 
     low = lax.broadcasted_iota(jnp.int32, (piece, LANES), 1) < members
 
     def packed(values):
         out = []
-        for k in range(chunks):
+        for k in range(values.shape[0] // late):
             base = 2 * piece * k
             out.append(jnp.where(low, values[base : base + piece], values[base + piece : base + 2 * piece]))
         return out
@@ -425,10 +445,9 @@
         east = jnp.where(lane == l, x[:, width - 1 : width], east)
     edge_w[...] = jnp.concatenate([west, west], axis=0).T[:8]
     edge_e[...] = jnp.concatenate([east, east], axis=0).T[:8]
-    for ref, k, l in ((part_u, 1, 0), (part_d, 2, depth - 1)):
+    for ref, k, edge, l in ((part_u, 2, depth - 1, 0), (part_d, 3, 0, depth - 1)):
         raw = jnp.concatenate(halves(cells[l]), axis=0)
-        for i, rows in enumerate(packed(doubled(dot_rows(found[k][2].astype(bf16), raw)))):
-            ref[i * piece : (i + 1) * piece, :] = rows
+        ref[...] = packed(doubled(dot_rows(facing(k, edge).astype(bf16), raw)))[0]
     pl.semaphore_wait(barrier, len(greeted))
 
     up, down = layer > 0, layer < layers - 1
@@ -449,13 +468,15 @@
     )
     for sends, receives, copy, place in small:
         pl.when(sends)(copy.start)
+    for sends, receives, copy, _ in large:
+        pl.when(sends)(copy.start)
     for sends, receives, copy, place in small + large:
 
         @pl.when(jnp.logical_not(receives))
         def _(place=place):
             place[...] = jnp.zeros_like(place)
 
-    at_row, at_col, hot = found[0]
+    at_row, at_col, hot = locate(cap, own)
     column = lax.broadcasted_iota(jnp.int32, (members, width), 1)
     total = jnp.zeros((cap, LANES), f32)
     for l in range(depth):
@@ -473,36 +494,42 @@
         picked = dot_rows(hot.astype(bf16), jnp.concatenate(halves(new), axis=0))
         total = total + jnp.where(at_row == l, picked, 0.0)
     mine = packed(doubled(total))
-    coef_u = diff_z[0:1, :] + 0.5 * cour_z[0:1, :]
-    coef_d = diff_z[depth - 1 : depth, :] - 0.5 * cour_z[depth - 1 : depth, :]
-    take_u = jnp.where(at_row == 0, jnp.sum(hot * coef_u, axis=1, keepdims=True), 0.0)
-    take_d = jnp.where(at_row == depth - 1, jnp.sum(hot * coef_d, axis=1, keepdims=True), 0.0)
-    coef_w = diff_x[:, 0:1] + 0.5 * cour_x[:, 0:1]
-    coef_e = diff_x[:, width - 1 : width] - 0.5 * cour_x[:, width - 1 : width]
-    weights = [packed(jnp.broadcast_to(take, (cap, LANES))) for take in (take_u, take_d)]
-    sides = []
-    for at, coef in ((0, coef_w), (width - 1, coef_e)):
-        for l in range(depth):
-            take = jnp.where(jnp.logical_and(at_row == l, at_col == at), coef[l : l + 1, :], 0.0)
-            sides.append(packed(jnp.broadcast_to(take, (cap, LANES))))
-
-    for sends, receives, copy, place in small:
-        pl.when(receives)(copy.wait_recv)
     me = (core * plane_n + spot) * line_n + line
     line_out, plane_out, core_out = ([[] for _ in range(chunks)] for _ in range(3))
-    for k in range(chunks):
-        rows = pl.ds(k * piece, piece)
-        value = mine[k] + weights[0][k] * near_u[rows, :] + weights[1][k] * near_d[rows, :]
-        for l in range(depth):
-            value = value + sides[l][k] * halo_w[l : l + 1, :] + sides[depth + l][k] * halo_e[l : l + 1, :]
+
+    def send_line(k, value):
         gathered[k, me] = value
         view = gathered.at[k, me]
         for j in range(1, line_n):
             copy = remote(view, view, line_send.at[k, j - 1], line_recv.at[k, j - 1], line_at((line + j) % line_n))
             copy.start()
             line_out[k].append(copy)
-    for sends, receives, copy, _ in large:
-        pl.when(sends)(copy.start)
+
+    for k in range(chunks - 1):
+        send_line(k, mine[k])
+    coef_u = diff_z[0:1, :] + 0.5 * cour_z[0:1, :]
+    coef_d = diff_z[depth - 1 : depth, :] - 0.5 * cour_z[depth - 1 : depth, :]
+    coef_w = diff_x[:, 0:1] + 0.5 * cour_x[:, 0:1]
+    coef_e = diff_x[:, width - 1 : width] - 0.5 * cour_x[:, width - 1 : width]
+    at_row, at_col, hot = at_row[cap - late :], at_col[cap - late :], hot[cap - late :]
+    take_u = jnp.where(at_row == 0, jnp.sum(hot * coef_u, axis=1, keepdims=True), 0.0)
+    take_d = jnp.where(at_row == depth - 1, jnp.sum(hot * coef_d, axis=1, keepdims=True), 0.0)
+
+    def spread_out(take):
+        return packed(jnp.broadcast_to(take, (late, LANES)))[0]
+
+    takes = [spread_out(take_u), spread_out(take_d)]
+    sides = []
+    for at, coef in ((0, coef_w), (width - 1, coef_e)):
+        for l in range(depth):
+            sides.append(spread_out(jnp.where(jnp.logical_and(at_row == l, at_col == at), coef[l : l + 1, :], 0.0)))
+
+    for sends, receives, copy, place in small:
+        pl.when(receives)(copy.wait_recv)
+    value = mine[chunks - 1] + takes[0] * near_u[...] + takes[1] * near_d[...]
+    for l in range(depth):
+        value = value + sides[l] * halo_w[l : l + 1, :] + sides[depth + l] * halo_e[l : l + 1, :]
+    send_line(chunks - 1, value)
 
     for ref, coef, at in ((halo_w, coef_w, 0), (halo_e, coef_e, width - 1)):
         base = at // LANES * LANES
@@ -516,6 +543,7 @@
         copy.wait()
     core_of, row_of, line_of = cell_tile & 1, divide(cell_tile, 2) & 1, divide(cell_tile, 4)
     owner = (core_of * plane_n + cell_layer * 2 + row_of) * line_n + line_of
+    owner = owner * 2 + rim.astype(jnp.int32)
     key = (owner * count + lax.broadcasted_iota(jnp.int32, (batches, count), 1)).astype(f32)
     upright = jnp.concatenate([key, jnp.zeros_like(key)], axis=0).T
 
@@ -533,12 +561,14 @@
     parts = []
     for values, n in fields:
         parts.extend(pieces(values, n))
-    devices_at = lax.broadcasted_iota(jnp.int32, (devices, count), 0)
+    holders = 2 * devices
+    devices_at = lax.broadcasted_iota(jnp.int32, (holders, count), 0)
     cuts_at = lax.broadcasted_iota(jnp.int32, (tiles * cuts, count), 0)
     ends = [divide(cell_col + obs_radius[...] * step, width // cuts) for step in (-1, 0, 1)]
-    used = jnp.zeros((devices, 1), f32)
+    used = jnp.zeros((holders, 1), f32)
+    begins = []
     worst = jnp.zeros((tiles * cuts, 1), f32)
-    longest = jnp.zeros((devices, 1), f32)
+    longest = jnp.zeros((holders, 1), f32)
     if len(parts) * batches % 16:
         parts.append(jnp.zeros((16 - len(parts) * batches % 16, count), f32))
     parts = jnp.concatenate(parts, axis=0).astype(bf16)
@@ -560,19 +590,28 @@
         start = jnp.sum(jnp.where(holder < devices_at, 1.0, 0.0), axis=1, keepdims=True)
         table[:, b : b + 1] = length.astype(jnp.int32)
         table[:, batches + b : batches + b + 1] = start.astype(jnp.int32)
-        table[:, 2 * batches + b : 2 * batches + b + 1] = used.astype(jnp.int32)
+        begins.append(used)
         used = used + length
         longest = jnp.maximum(longest, length)
         bent = jnp.zeros((tiles * cuts, count), f32)
         for end in ends:
             bent = bent + jnp.where(end[b : b + 1, :] == cuts_at, 1.0, 0.0)
         worst = jnp.maximum(worst, jnp.sum(bent, axis=1, keepdims=True))
-    longest = jnp.max(longest, axis=0, keepdims=True)
-    table[:, 3 * batches : 3 * batches + 1] = jnp.broadcast_to(longest, (devices, 1)).astype(jnp.int32)
-    over = jnp.logical_or(jnp.max(used) > cap, jnp.max(worst) > bends)
+    odd = lax.broadcasted_iota(jnp.int32, (holders, 1), 0) % 2
+    end = jnp.where(odd == 1, cap - used, 0.0)
+    for b in range(batches):
+        table[:, 2 * batches + b : 2 * batches + b + 1] = (begins[b] + end).astype(jnp.int32)
+    for i in range(2):
+        most = jnp.max(jnp.where(odd == i, longest, 0.0), axis=0, keepdims=True)
+        table[:, 3 * batches + i : 3 * batches + i + 1] = jnp.broadcast_to(most, (holders, 1)).astype(jnp.int32)
+    inner = jnp.broadcast_to(jnp.where(odd == 0, used, 0.0), (holders, LANES))
+    pair_of = jnp.broadcast_to(used, (holders, LANES))
+    room = jnp.where(odd == 1, pltpu.roll(inner, 1, 0) + pair_of, 0.0)
+    rim_most = jnp.max(jnp.where(odd == 1, used, 0.0))
+    over = jnp.logical_or(jnp.max(room) > cap, jnp.logical_or(rim_most > late, jnp.max(worst) > bends))
     flag[0] = over.astype(jnp.int32)
 
-    for k in range(chunks):
+    def send_plane(k):
         for copy in line_out[k]:
             copy.wait_recv()
         view = gathered.at[k, pl.ds((core * plane_n + spot) * line_n, line_n)]
@@ -580,6 +619,9 @@
             copy = remote(view, view, plane_send.at[k, j - 1], plane_recv.at[k, j - 1], plane_at((spot + j) % plane_n))
             copy.start()
             plane_out[k].append(copy)
+
+    for k in range(chunks - 1):
+        send_plane(k)
 
     part_w = width // cuts
     middle = (part_w - 1) / 2
@@ -631,6 +673,7 @@
             tapers[i] = bump(centre[c : c + 1, :], upright[:, b : b + 1], upright[:, batches + b : batches + b + 1])
             i += 1
 
+    send_plane(chunks - 1)
     for sends, receives, copy, _ in large:
         pl.when(receives)(copy.wait_recv)
     state[0] += halo_u[...] * coef_u
@@ -673,25 +716,27 @@
     load.start()
     depth, members, _ = layers_ref.shape
     batches, _, count = later_ref.shape
-    devices = table.shape[0]
+    devices = table.shape[0] // 2
     mean = count / devices
     run = min(cap, -int(-(mean + 4.0 * mean**0.5) // 8) * 8)
-
-    def spread(size):
+    short = max(8, run // 16 * 8)
+
+    def spread(sizes):
         def step(g, carry):
             for b in range(batches):
-                dst, src = table[g, batches + b], g * cap + table[g, 2 * batches + b]
-                for i in range(0, size, 8):
-                    ordered[b, pl.ds(dst + i, 8), :] = flat[pl.ds(src + i, 8), :]
+                for i in range(2):
+                    dst, src = table[2 * g + i, batches + b], g * cap + table[2 * g + i, 2 * batches + b]
+                    for at in range(0, sizes[i], 8):
+                        ordered[b, pl.ds(dst + at, 8), :] = flat[pl.ds(src + at, 8), :]
             return carry
 
         return step
 
-    lax.fori_loop(0, devices, spread(run), 0, unroll=4)
-
-    @pl.when(table[0, 3 * batches] > run)
+    lax.fori_loop(0, devices, spread((run, short)), 0, unroll=4)
+
+    @pl.when(jnp.logical_or(table[0, 3 * batches] > run, table[0, 3 * batches + 1] > short))
     def _():
-        lax.fori_loop(0, devices, spread(cap), 0)
+        lax.fori_loop(0, devices, spread((cap, cap)), 0)
 
     for b in range(batches):
         later_ref[b] = ordered[b, :count, :].T[:members]
@@ -732,15 +777,6 @@
 
         if b < batches - 1:
             lhs = twice(jnp.concatenate([y_high, y_low], axis=0).T)
-        rest = range(b + 1, batches)
-        crosses = [jnp.dot(lhs, stack(later_ref[c]), preferred_element_type=jnp.float32) for c in rest]
-        gains = [halves(cross * tapers[pair + i]) for i, cross in enumerate(crosses)]
-        pair += len(rest)
-        ones = [jnp.dot(d_both, high, preferred_element_type=jnp.float32) for high, _ in gains]
-        twos = [jnp.dot(d_high, lower, preferred_element_type=jnp.float32) for _, lower in gains]
-        for i, c in enumerate(rest):
-            later_ref[c] += ones[i][:members] + ones[i][members:] + twos[i]
-
         scaled = []
         for c in range(cuts):
             for i in range(3):
@@ -772,6 +808,15 @@
             right = right.astype(jnp.bfloat16)
             lefts.append(left)
             rights.append(right)
+        rest = range(b + 1, batches)
+        crosses = [jnp.dot(lhs, stack(later_ref[c]), preferred_element_type=jnp.float32) for c in rest]
+        splits = [halves(cross * tapers[pair + i]) for i, cross in enumerate(crosses)]
+        pair += len(rest)
+        ones = [jnp.dot(d_both, high, preferred_element_type=jnp.float32) for high, _ in splits]
+        twos = [jnp.dot(d_high, lower, preferred_element_type=jnp.float32) for _, lower in splits]
+        for i, c in enumerate(rest):
+            later_ref[c] += ones[i][:members] + ones[i][members:] + twos[i]
+
         olds, firsts, gains, seconds = [], [], [], []
         for c in range(cuts):
             columns = slice(c * part_w, (c + 1) * part_w)
@@ -881,7 +926,7 @@
             jax.ShapeDtypeStruct((cuts * 4 * batches, count), f32),
             jax.ShapeDtypeStruct((batches, cuts, bends, width // cuts), f32),
             jax.ShapeDtypeStruct((batches * (batches - 1) // 2, count, count), f32),
-            jax.ShapeDtypeStruct((devices, 3 * batches + 1), jnp.int32),
+            jax.ShapeDtypeStruct((2 * devices, 3 * batches + 2), jnp.int32),
             jax.ShapeDtypeStruct((1,), jnp.int32),
         ),
         in_specs=[hbm] * 9,
@@ -896,7 +941,7 @@
             dma((9,)),
             pltpu.VMEM((depth, members, width), f32),
             *[pltpu.VMEM((8, LANES), f32)] * 4,
-            *[pltpu.VMEM((cap // 2, LANES), f32)] * 4,
+            *[pltpu.VMEM((piece, LANES), f32)] * 4,
             *[pltpu.VMEM((members, width), f32)] * 2,
             pltpu.VMEM((chunks, devices, piece, LANES), f32),
             dma((6,)),

time: 29.2 us -> 28.2 us (0.966)
  Pallas kernels: 27.9 us -> 27 us
    pallas_call x1, Pallas kernels: 19.6 us -> 18.2 us  [shards(): pl.pallas_call(functools.partial(collect_kernel, tiles, layers, cap, cuts...]
    pallas_call x1, Pallas kernels: 8.31 us -> 8.73 us  [fast(): pl.pallas_call(functools.partial(apply_kernel, cap), out_shape=jax.ShapeD...]
where the time goes in v4:
time: 28.2 us; the launch traced here: 28 us
  Pallas kernels  27 us (96%)
  between operations  0.81 us (3%)
    pallas_call x1, Pallas kernels, shards(): pl.pallas_call(functools.partial(collect_kernel, tiles, layers, cap, cuts...  18.2 us
    pallas_call x1, Pallas kernels, fast(): pl.pallas_call(functools.partial(apply_kernel, cap), out_shape=jax.ShapeD...  8.73 us

profile of v4, /device:TPU:1, one launch (start us, length us, event | category | flops | bytes accessed | tf_op | source)
XLA Modules:
  0.0 28.0 jit_solution(9429238661145118205)
XLA Ops:
  0.0 18.2 %collect.1 = (f32[4,64,512]{2,1,0:T(8,128)S(1)}, f32[3168,128]{1,0:T(8,128)S(1)}, f32[16,512]{1,0:T(8,128)S(1)}, f32[32,512]{1,0:T(8,128)S(1)}, f32[4,2,64,256]{...) custom-call(f32[64,4,512]{2,1,0:T(4,128)} %ens_in.1, f32[4,512]{1,0:T(4,128)} %dx_in.1, ...), custom_call_target="tpu_custom_call" | custom-call | tf_op jit(solution)/shard_map/collect/pallas_call | solution.py:920
  18.9 9.0 %conditional.1 = (f32[64,4,512]{2,1,0:T(4,128)}) conditional(s32[]{:T(128)} %bitcast, (s32[64,14]{1,0:T(8,128)S(1)}, f32[4,64,512]{2,1,0:T(8,128)S(1)}, f32[3168,128]{1,0:T(8,128)S(1)}, f32[16,512]{1,0:T(8,128)S(1)}, f32[32,512]{1,0:T(8,128)S(1)}, /*index=5*/f32[4,2,64,256]{3,2,1,0:T(8,128)S(1)}, f32[6,512,512]{2,1,0:T(8,128)S(1)}) %tuple.11, ...), branch_computations={%region_0.0_spmd, %region_1.0_spmd} | conditional | bytes 8 | solution.py:976
  18.9 8.7 %apply.1 = f32[64,4,512]{2,1,0:T(4,128)} custom-call(s32[64,14]{1,0:T(8,128)S(1)} %get-tuple-element.40.table, f32[4,64,512]{2,1,0:T(8,128)S(1)} %get-tuple-element.41.state_in, f32[3168,128]{1,0:T(8,128)S(1)} %get-tuple-element.42.flat, f32[16,512]{1,0:T(8,128)S(1)} %get-tuple-element.43.meta, f32[32,512]{1,0:T(8,128)S(1)} %get-tuple-element.44.taper_in, ...), custom_call_target="tpu_custom_call" | custom-call | tf_op jit(solution)/shard_map/cond/branch_0_fun/apply/pallas_call | solution.py:958

commit v5 on v4

--- a/solution.py
+++ b/solution.py
@@ -566,7 +566,7 @@
     cuts_at = lax.broadcasted_iota(jnp.int32, (tiles * cuts, count), 0)
     ends = [divide(cell_col + obs_radius[...] * step, width // cuts) for step in (-1, 0, 1)]
     used = jnp.zeros((holders, 1), f32)
-    begins = []
+    begins, starts = [], []
     worst = jnp.zeros((tiles * cuts, 1), f32)
     longest = jnp.zeros((holders, 1), f32)
     if len(parts) * batches % 16:
@@ -588,8 +588,7 @@
         holder = owner[b : b + 1, :]
         length = jnp.sum(jnp.where(holder == devices_at, 1.0, 0.0), axis=1, keepdims=True)
         start = jnp.sum(jnp.where(holder < devices_at, 1.0, 0.0), axis=1, keepdims=True)
-        table[:, b : b + 1] = length.astype(jnp.int32)
-        table[:, batches + b : batches + b + 1] = start.astype(jnp.int32)
+        starts.append(start)
         begins.append(used)
         used = used + length
         longest = jnp.maximum(longest, length)
@@ -599,11 +598,17 @@
         worst = jnp.maximum(worst, jnp.sum(bent, axis=1, keepdims=True))
     odd = lax.broadcasted_iota(jnp.int32, (holders, 1), 0) % 2
     end = jnp.where(odd == 1, cap - used, 0.0)
-    for b in range(batches):
-        table[:, 2 * batches + b : 2 * batches + b + 1] = (begins[b] + end).astype(jnp.int32)
+    entries = starts + [begin + end for begin in begins]
     for i in range(2):
         most = jnp.max(jnp.where(odd == i, longest, 0.0), axis=0, keepdims=True)
-        table[:, 3 * batches + i : 3 * batches + i + 1] = jnp.broadcast_to(most, (holders, 1)).astype(jnp.int32)
+        entries.append(jnp.broadcast_to(most, (holders, 1)))
+    entry_lane = lax.broadcasted_iota(jnp.int32, (holders, LANES), 1)
+    listed = jnp.zeros((holders, LANES), f32)
+    for i, entry in enumerate(entries):
+        listed = jnp.where(entry_lane == i, entry, listed)
+    if holders % LANES:
+        listed = jnp.concatenate([listed, jnp.zeros((-holders % LANES, LANES), f32)], axis=0)
+    table[...] = listed.T[: table.shape[0]].astype(jnp.int32)
     inner = jnp.broadcast_to(jnp.where(odd == 0, used, 0.0), (holders, LANES))
     pair_of = jnp.broadcast_to(used, (holders, LANES))
     room = jnp.where(odd == 1, pltpu.roll(inner, 1, 0) + pair_of, 0.0)
@@ -710,13 +715,12 @@
 
 
 def apply_kernel(
-    cap, table, state_in, flat, meta, taper_in, kinks, tapers, out, layers_ref, later_ref, ordered, load_sem,
+    cap, devices, table, state_in, flat, meta, taper_in, kinks, tapers, out, layers_ref, later_ref, ordered, load_sem,
 ):
     load = pltpu.make_async_copy(state_in, layers_ref, load_sem)
     load.start()
     depth, members, _ = layers_ref.shape
     batches, _, count = later_ref.shape
-    devices = table.shape[0] // 2
     mean = count / devices
     run = min(cap, -int(-(mean + 4.0 * mean**0.5) // 8) * 8)
     short = max(8, run // 16 * 8)
@@ -725,7 +729,7 @@
         def step(g, carry):
             for b in range(batches):
                 for i in range(2):
-                    dst, src = table[2 * g + i, batches + b], g * cap + table[2 * g + i, 2 * batches + b]
+                    dst, src = table[b, 2 * g + i], g * cap + table[batches + b, 2 * g + i]
                     for at in range(0, sizes[i], 8):
                         ordered[b, pl.ds(dst + at, 8), :] = flat[pl.ds(src + at, 8), :]
             return carry
@@ -734,7 +738,7 @@
 
     lax.fori_loop(0, devices, spread((run, short)), 0, unroll=4)
 
-    @pl.when(jnp.logical_or(table[0, 3 * batches] > run, table[0, 3 * batches + 1] > short))
+    @pl.when(jnp.logical_or(table[2 * batches, 0] > run, table[2 * batches + 1, 0] > short))
     def _():
         lax.fori_loop(0, devices, spread((cap, cap)), 0)
 
@@ -911,7 +915,7 @@
     cap = -int(-(mean + 4.0 * mean**0.5) // 16) * 16
     piece = 16 if cap % 32 == 0 else 8
     chunks = cap // (2 * piece)
-    cuts, bends = (2, 64) if width % (2 * LANES) == 0 else (1, LANES)
+    cuts, bends = 1, LANES
     vmem = pl.BlockSpec(memory_space=pltpu.VMEM)
     smem = pl.BlockSpec(memory_space=pltpu.SMEM)
     hbm = pl.BlockSpec(memory_space=pltpu.HBM)
@@ -926,7 +930,7 @@
             jax.ShapeDtypeStruct((cuts * 4 * batches, count), f32),
             jax.ShapeDtypeStruct((batches, cuts, bends, width // cuts), f32),
             jax.ShapeDtypeStruct((batches * (batches - 1) // 2, count, count), f32),
-            jax.ShapeDtypeStruct((2 * devices, 3 * batches + 2), jnp.int32),
+            jax.ShapeDtypeStruct((-(-(2 * batches + 2) // 8) * 8, -(-2 * devices // LANES) * LANES), jnp.int32),
             jax.ShapeDtypeStruct((1,), jnp.int32),
         ),
         in_specs=[hbm] * 9,
@@ -956,7 +960,7 @@
 
     def fast():
         return pl.pallas_call(
-            functools.partial(apply_kernel, cap),
+            functools.partial(apply_kernel, cap, devices),
             out_shape=jax.ShapeDtypeStruct((members, depth, width), f32),
             in_specs=[smem, hbm, vmem, vmem, vmem, vmem, vmem],
             out_specs=vmem,

time: 28.2 us -> 28 us (level)
  Pallas kernels: 27 us -> 26.7 us
    pallas_call x1, Pallas kernels: 8.73 us -> 8.4 us  [fast(): pl.pallas_call(functools.partial(apply_kernel, cap, devices), out_shape=j...]
where the time goes in v5:
time: 28 us; the launch traced here: 27.7 us
  Pallas kernels  26.7 us (95%)
  between operations  0.81 us (3%)
    pallas_call x1, Pallas kernels, shards(): pl.pallas_call(functools.partial(collect_kernel, tiles, layers, cap, cuts...  18.3 us
    pallas_call x1, Pallas kernels, fast(): pl.pallas_call(functools.partial(apply_kernel, cap, devices), out_shape=j...  8.4 us

profile of v5, /device:TPU:1, one launch (start us, length us, event | category | flops | bytes accessed | tf_op | source)
XLA Modules:
  0.0 27.7 jit_solution(18013995386578608751)
XLA Ops:
  0.0 18.3 %collect.1 = (f32[4,64,512]{2,1,0:T(8,128)S(1)}, f32[3168,128]{1,0:T(8,128)S(1)}, f32[16,512]{1,0:T(8,128)S(1)}, f32[16,512]{1,0:T(8,128)S(1)}, f32[4,1,128,512]...) custom-call(f32[64,4,512]{2,1,0:T(4,128)} %ens_in.1, f32[4,512]{1,0:T(4,128)} %dx_in.1, ...), custom_call_target="tpu_custom_call" | custom-call | tf_op jit(solution)/shard_map/collect/pallas_call | solution.py:924
  18.9 8.6 %conditional.1 = (f32[64,4,512]{2,1,0:T(4,128)}) conditional(s32[]{:T(128)} %bitcast, (s32[16,128]{1,0:T(8,128)S(1)}, f32[4,64,512]{2,1,0:T(8,128)S(1)}, f32[3168,128]{1,0:T(8,128)S(1)}, f32[16,512]{1,0:T(8,128)S(1)}, f32[16,512]{1,0:T(8,128)S(1)}, /*index=5*/f32[4,1,128,512]{3,2,1,0:T(8,128)S(1)}, f32[6,512,512]{2,1,0:T(8,128)S(1)}) %tuple.11, ...), branch_computations={%region_0.0_spmd, %region_1.0_spmd} | conditional | bytes 8 | solution.py:980
  18.9 8.4 %apply.1 = f32[64,4,512]{2,1,0:T(4,128)} custom-call(s32[16,128]{1,0:T(8,128)S(1)} %get-tuple-element.40.table, f32[4,64,512]{2,1,0:T(8,128)S(1)} %get-tuple-element.41.state_in, f32[3168,128]{1,0:T(8,128)S(1)} %get-tuple-element.42.flat, f32[16,512]{1,0:T(8,128)S(1)} %get-tuple-element.43.meta, f32[16,512]{1,0:T(8,128)S(1)} %get-tuple-element.44.taper_in, ...), custom_call_target="tpu_custom_call" | custom-call | tf_op jit(solution)/shard_map/cond/branch_0_fun/apply/pallas_call | solution.py:962

commit v6 on v5

--- a/solution.py
+++ b/solution.py
@@ -445,9 +445,15 @@
         east = jnp.where(lane == l, x[:, width - 1 : width], east)
     edge_w[...] = jnp.concatenate([west, west], axis=0).T[:8]
     edge_e[...] = jnp.concatenate([east, east], axis=0).T[:8]
-    for ref, k, edge, l in ((part_u, 2, depth - 1, 0), (part_d, 3, 0, depth - 1)):
-        raw = jnp.concatenate(halves(cells[l]), axis=0)
-        ref[...] = packed(doubled(dot_rows(facing(k, edge).astype(bf16), raw)))[0]
+    for there, ref, k, edge, l in (
+        (layer > 0, part_u, 2, depth - 1, 0), (layer < layers - 1, part_d, 3, 0, depth - 1)
+    ):
+
+        @pl.when(there)
+        def _(ref=ref, k=k, edge=edge, l=l):
+            raw = jnp.concatenate(halves(cells[l]), axis=0)
+            ref[...] = packed(doubled(dot_rows(facing(k, edge).astype(bf16), raw)))[0]
+
     pl.semaphore_wait(barrier, len(greeted))
 
     up, down = layer > 0, layer < layers - 1

time: 28 us -> 28 us (level)
  no operation moved by 1% of the time
where the time goes in v6:
time: 28 us; the launch traced here: 27.8 us
  Pallas kernels  26.8 us (96%)
  between operations  0.81 us (3%)
    pallas_call x1, Pallas kernels, shards(): pl.pallas_call(functools.partial(collect_kernel, tiles, layers, cap, cuts...  18.4 us
    pallas_call x1, Pallas kernels, fast(): pl.pallas_call(functools.partial(apply_kernel, cap, devices), out_shape=j...  8.4 us

profile of v6, /device:TPU:1, one launch (start us, length us, event | category | flops | bytes accessed | tf_op | source)
XLA Modules:
  0.0 27.8 jit_solution(15960303595218708058)
XLA Ops:
  0.0 18.4 %collect.1 = (f32[4,64,512]{2,1,0:T(8,128)S(1)}, f32[3168,128]{1,0:T(8,128)S(1)}, f32[16,512]{1,0:T(8,128)S(1)}, f32[16,512]{1,0:T(8,128)S(1)}, f32[4,1,128,512]...) custom-call(f32[64,4,512]{2,1,0:T(4,128)} %ens_in.1, f32[4,512]{1,0:T(4,128)} %dx_in.1, ...), custom_call_target="tpu_custom_call" | custom-call | tf_op jit(solution)/shard_map/collect/pallas_call | solution.py:930
  19.0 8.6 %conditional.1 = (f32[64,4,512]{2,1,0:T(4,128)}) conditional(s32[]{:T(128)} %bitcast, (s32[16,128]{1,0:T(8,128)S(1)}, f32[4,64,512]{2,1,0:T(8,128)S(1)}, f32[3168,128]{1,0:T(8,128)S(1)}, f32[16,512]{1,0:T(8,128)S(1)}, f32[16,512]{1,0:T(8,128)S(1)}, /*index=5*/f32[4,1,128,512]{3,2,1,0:T(8,128)S(1)}, f32[6,512,512]{2,1,0:T(8,128)S(1)}) %tuple.11, ...), branch_computations={%region_0.0_spmd, %region_1.0_spmd} | conditional | bytes 8 | solution.py:986
  19.0 8.4 %apply.1 = f32[64,4,512]{2,1,0:T(4,128)} custom-call(s32[16,128]{1,0:T(8,128)S(1)} %get-tuple-element.40.table, f32[4,64,512]{2,1,0:T(8,128)S(1)} %get-tuple-element.41.state_in, f32[3168,128]{1,0:T(8,128)S(1)} %get-tuple-element.42.flat, f32[16,512]{1,0:T(8,128)S(1)} %get-tuple-element.43.meta, f32[16,512]{1,0:T(8,128)S(1)} %get-tuple-element.44.taper_in, ...), custom_call_target="tpu_custom_call" | custom-call | tf_op jit(solution)/shard_map/cond/branch_0_fun/apply/pallas_call | solution.py:968
